TPU v7x, 256 devices: a whole 4x4x8 slice. The times are simulated.
256 devices in a mesh: section: 4 (over x_hi, core), tensor: 8 (over z), dp: 8 (over x_lo, y).
Axes of the slice: x: 4 (x_hi: 2, x_lo: 2; x = x_hi * 2 + x_lo), y: 4, z: 8, core: 2. Of those that a mesh axis runs over, the one named last changes fastest.
Arguments:
- act_inbox: bfloat16 [4, 4096, 16384], P('section', 'dp', 'tensor'), may hold values from -6 to 6
- grad_inbox: bfloat16 [4, 4096, 16384], P('section', 'dp', 'tensor'), may hold values from -0.0625 to 0.0625
- queries: bfloat16 [4, 4096, 16384], P('section', 'dp', 'tensor'), may hold values from -400 to 400
- keys_values: bfloat16 [4, 2, 4096, 1024], P('section', None, 'dp', 'tensor'), may hold values from -6 to 6
- saved_attn: bfloat16 [4, 4096, 16384], P('section', 'dp', 'tensor'), may hold values from -6 to 6
- down_adapt: bfloat16 [4, 8, 16, 16384], P('section', None, None, 'tensor'), may hold values from -0.375 to 0.375
- up_adapt: bfloat16 [4, 8, 16, 16384], P('section', None, None, 'tensor'), may hold values from -0.75 to 0.75
- seg_blocks: int32 [4, 2, 8, 3], P('section', None, 'dp'), may hold values from 1 to 4, 8 in all within a row
- seg_pads: int32 [4, 2, 8, 3], P('section', None, 'dp'), may hold values from 0 to 63
- seg_tenant: int32 [4, 2, 8, 3], P('section', None, 'dp'), may hold values from 0 to 31
- adapter_table: int32 [32], replicated, may hold values from 0 to 7
Outputs:
- new_acts: bfloat16 [4, 4096, 16384], P('section', 'dp', 'tensor')
- grad_down: bfloat16 [4, 8, 16, 16384], P('section', None, None, 'tensor')
- grad_up: bfloat16 [4, 8, 16, 16384], P('section', None, None, 'tensor')
Inputs may be any that keep to these rules, and one draw needn't show every extreme that they name: `seg_blocks`: each row of 3 block counts sums to 8.
All inputs are finite; a program needn't handle non-finite values.
Results may differ from a plain program's by a relative error of at most 0.0058.
Values may be sent and summed in bfloat16 or wider, within the bound.
No kernel may reach another device: no remote copies, remote signals or barrier semaphores. Data moves between devices by JAX's collectives and lax.ppermute only.
A program may use at most 128 MiB of HBM per device.

v0:
```python
import math

import jax
import jax.numpy as jnp
from jax import lax
from jax.sharding import PartitionSpec as P

HD = 128
BLOCK = 64


adapter_scale = 2.0


def from_behind(value, axis, steps):
    count = lax.axis_size(axis)
    pairs = [(source, (source + steps) % count) for source in range(count)]
    return lax.ppermute(value, axis, pairs)


def token_layout(blocks, padding, tenants, slot_table, length, slot_count):
    positions = jnp.arange(length, dtype=jnp.int32)
    seg_ends = jnp.cumsum(blocks) * BLOCK
    segment = jnp.sum((positions[:, None] >= seg_ends[None, :]).astype(jnp.int32), axis=1)
    member = (segment[:, None] == jnp.arange(blocks.shape[0], dtype=jnp.int32)[None, :]).astype(
        jnp.int32
    )
    live_end = jnp.sum(member * (seg_ends - padding)[None, :], axis=1)
    alive = positions < live_end
    tenant_pick = (
        tenants[:, None] == jnp.arange(slot_table.shape[0], dtype=jnp.int32)[None, :]
    ).astype(jnp.int32)
    seg_slot = jnp.sum(tenant_pick * slot_table[None, :], axis=1)
    token_slot = jnp.sum(member * seg_slot[None, :], axis=1)
    onehot = (token_slot[:, None] == jnp.arange(slot_count, dtype=jnp.int32)[None, :]).astype(
        jnp.float32
    )
    return (segment, alive, onehot)


def attend(queries, keys_values, segment, alive):
    length = queries.shape[0]
    kv_width = keys_values.shape[-1]
    kv_heads = kv_width // HD
    group_size = queries.shape[1] // kv_width
    query_heads = queries.reshape(length, kv_heads, group_size, HD)
    key_heads = keys_values[0].reshape(length, kv_heads, HD)
    value_heads = keys_values[1].reshape(length, kv_heads, HD)
    positions = jnp.arange(length, dtype=jnp.int32)
    inv_root = 1.0 / math.sqrt(HD)

    def one_block(block_index):
        block_start = block_index * length
        block_pos = block_start + jnp.arange(length, dtype=jnp.int32)
        scores = (
            jnp.einsum("qhgd,khd->hgqk", query_heads, key_heads, preferred_element_type=jnp.float32)
            * inv_root
        )
        allowed = (segment[:, None] == segment[None, :]) & (
            block_pos[:, None] >= positions[None, :]
        )
        allowed = allowed & alive[None, :] & alive[:, None]
        masked_scores = jnp.where(allowed, scores, -1e30)
        row_top = jnp.max(masked_scores, axis=-1, keepdims=True)
        exponent = jnp.where(allowed, jnp.exp(masked_scores - row_top), 0.0)
        row_total = jnp.sum(exponent, axis=-1, keepdims=True)
        row_total = jnp.where(alive[None, None, :, None], row_total, 1.0)
        weights = (exponent / row_total).astype(jnp.bfloat16)
        attended = jnp.einsum(
            "hgqk,khd->qhgd", weights, value_heads, preferred_element_type=jnp.float32
        )
        return attended.astype(jnp.bfloat16).reshape(length, kv_heads * group_size * HD)

    blocks_out = lax.map(one_block, jnp.arange(length // length, dtype=jnp.int32))
    return blocks_out.reshape(length, -1)


def project_rows(left, right):
    return lax.dot_general(
        left, right, (((1,), (1,)), ((), ())), preferred_element_type=jnp.float32
    )


def contract(left, right):
    return lax.dot_general(
        left, right, (((0,), (0,)), ((), ())), preferred_element_type=jnp.float32
    )


def select_slots(full, onehot):
    return jnp.sum(full.reshape(full.shape[0], onehot.shape[1], -1) * onehot[:, :, None], axis=1)


def spread_tokens(ranked, onehot):
    wide = onehot[:, :, None] * ranked.astype(jnp.float32)[:, None, :]
    return wide.reshape(ranked.shape[0], -1).astype(jnp.bfloat16)


def per_device(
    act_inbox,
    grad_inbox,
    queries,
    keys_values,
    saved_attn,
    down_adapt,
    up_adapt,
    seg_blocks,
    seg_pads,
    seg_tenant,
    adapter_table,
):
    received_input = from_behind(act_inbox[0], "section", 1)
    returned = from_behind(grad_inbox[0], "section", -1)
    length = received_input.shape[0]
    slot_count = up_adapt.shape[1]
    down_rows = down_adapt[0].reshape(-1, down_adapt.shape[-1])
    upward_rows = up_adapt[0].reshape(-1, up_adapt.shape[-1])
    segment, alive, onehot = token_layout(
        seg_blocks[0, 0, 0],
        seg_pads[0, 0, 0],
        seg_tenant[0, 0, 0],
        adapter_table,
        length,
        slot_count,
    )
    back_seg, back_alive, backward_slot_mask = token_layout(
        seg_blocks[0, 1, 0],
        seg_pads[0, 1, 0],
        seg_tenant[0, 1, 0],
        adapter_table,
        length,
        slot_count,
    )
    saved_rows = saved_attn[0]
    masked_scores = returned * back_alive[:, None].astype(jnp.bfloat16)
    back_part = select_slots(project_rows(saved_rows, down_rows), backward_slot_mask)
    grad_part = select_slots(project_rows(masked_scores, upward_rows), backward_slot_mask)
    attended = attend(queries[0], keys_values[0], segment, alive)
    fwd_part = select_slots(project_rows(attended, down_rows), onehot)
    back_sum, gradient_total = lax.psum((back_part, grad_part), "tensor")
    fwd_sum = lax.psum(fwd_part, "tensor")
    adapter_update = jnp.dot(
        spread_tokens(fwd_sum.astype(jnp.bfloat16), onehot),
        upward_rows,
        preferred_element_type=jnp.float32,
    )
    summed_output = received_input.astype(jnp.float32) + adapter_scale * adapter_update
    new_acts = summed_output.astype(jnp.bfloat16)
    spread_rank = spread_tokens(back_sum.astype(jnp.bfloat16), backward_slot_mask)
    spread_gradient = spread_tokens(
        (adapter_scale * gradient_total).astype(jnp.bfloat16), backward_slot_mask
    )
    grad_d, up_gradient = lax.psum(
        (contract(spread_gradient, saved_rows), contract(spread_rank, masked_scores)), "dp"
    )
    output_layout = up_adapt.shape
    return (
        new_acts[None],
        grad_d.reshape(output_layout).astype(jnp.bfloat16),
        (adapter_scale * up_gradient).reshape(output_layout).astype(jnp.bfloat16),
    )


def solution(mesh):
    placed = (
        P("section", "dp", "tensor"),
        P("section", "dp", "tensor"),
        P("section", "dp", "tensor"),
        P("section", None, "dp", "tensor"),
        P("section", "dp", "tensor"),
        P("section", None, None, "tensor"),
        P("section", None, None, "tensor"),
        P("section", None, "dp", None),
        P("section", None, "dp", None),
        P("section", None, "dp", None),
        P(),
    )
    return jax.shard_map(
        per_device,
        mesh=mesh,
        in_specs=placed,
        out_specs=(
            P("section", "dp", "tensor"),
            P("section", None, None, "tensor"),
            P("section", None, None, "tensor"),
        ),
        check_vma=False,
    )
```

profile of v0, /device:TPU:1, one launch (start us, length us, event | category | flops | bytes accessed | tf_op | source)
XLA Modules:
  0.0 180.9 jit_solution(15946681228733129986)
XLA Ops:
  7.2 0.0 copy-start
  7.2 0.0 all-reduce.5.cloned.1.call-start
  7.2 3.3 %collective-permute-start.1 = (bf16[512,2048]{1,0:T(8,128)(2,1)}, bf16[512,2048]{1,0:T(8,128)(2,1)}, u32[]{:S(2)}, u32[]{:S(2)}) collective-permute-start(bf16[512,2048]{1,0:T(8,128)(2,1)} %bitcast.115), channel_id=1, source_target_pairs={{0,192},{64,0},{128,64},{192,128},{1,193},{65,1},{129,65},{193,129... | collective-permute-start | bytes 6291464 | tf_op jit(solution)/shard_map/ppermute | solution.py:18
  10.6 1.0 collective-permute-start
  11.5 0.7 slice_bitcast_fusion.1
  12.2 0.2 reduce-window.14
  12.4 0.2 reduce-window.15
  12.6 0.7 bitcast_subtract_fusion
  13.2 0.1 convert_reduce_fusion.1
  13.3 0.7 slice_bitcast_fusion.2
  14.0 0.1 convert_reduce_fusion
  14.1 0.9 select_reduce_fusion.4
  15.0 0.1 select_reduce_fusion.1
  15.1 0.2 fusion.37
  15.3 2.2 %copy.26 = bf16[64,8,16,128]{3,2,1,0:T(8,128)(2,1)S(1)} copy(bf16[64,8,16,128]{3,1,2,0:T(8,128)(2,1)} %bitcast.108) | data formatting | bytes 4194304
  17.6 3.9 %fusion = (f32[16,512]{1,0:T(8,128)S(1)}, f32[512,512,16]{1,0,2:T(8,128)S(1)}) fusion(pred[512,512]{0,1:T(8,128)(4,1)S(1)} %fusion.37, bf16[512,16,128]{2,1,0:T(8,128)(2,1)S(1)} %bitcast.107, bf16[1,2,512,128]{3,2,1,0:T(8,128)(2,1)S(1)} %copy-done.2), kind=kOutput, calls=%fused_computation.3 | convolution fusion | flops 1086316544 | bytes 19300352 | tf_op jit(solution)/shard_map/while/body/eval_jaxpr/qhgd,khd->hgqk/dot_general | solution.py:56
  21.4 4.0 %fusion.1 = f32[16,512]{1,0:T(8,128)S(1)} fusion(f32[512,512,16]{1,0,2:T(8,128)S(1)} %get-tuple-element.45, f32[16,512]{1,0:T(8,128)S(1)} %get-tuple-element.44, pred[512,512]{0,1:T(8,128)(4,1)S(1)} %fusion.37), kind=kLoop, calls=%fused_computation.4 | loop fusion | flops 20963328 | bytes 17104896 | tf_op jit(solution)/shard_map/while/body/eval_jaxpr/reduce_sum | solution.py:66
  25.5 0.0 copy-start.3
  25.5 5.6 %fusion.14 = bf16[16,512,128]{1,2,0:T(8,128)(2,1)S(1)} fusion(f32[16,512]{1,0:T(8,128)S(1)} %broadcast_select_fusion, f32[16,512]{1,0:T(8,128)S(1)} %get-tuple-element.44, f32[512,512,16]{1,0,2:T(8,128)S(1)} %get-tuple-element.45, pred[512,512]{0,1:T(8,128)(4,1)S(1)} %fusion.37, bf16[1,2,512,128]{3,2,1,0:T(8,128)(2,1)S(1)} %copy-done.2), kind=kOutput, calls=%fused_computation.18 | convolution fusion | flops 1099956224 | bytes 19333120 | tf_op jit(solution)/shard_map/while/body/eval_jaxpr/hgqk,khd->qhgd/dot_general | solution.py:69
  31.1 0.5 fusion.26
  31.6 0.0 copy-start.1
  31.6 0.8 fusion.27
  32.5 23.3 %collective-permute-done.1 = bf16[512,2048]{1,0:T(8,128)(2,1)} collective-permute-done((bf16[512,2048]{1,0:T(8,128)(2,1)}, bf16[512,2048]{1,0:T(8,128)(2,1)}, u32[]{:S(2)}, u32[]{:S(2)}) %collective-permute-start.1) | collective-permute-done | bytes 2097184 | tf_op jit(solution)/shard_map/ppermute | solution.py:18
  55.8 2.5 %fusion.30 = f32[512,16]{0,1:T(8,128)S(1)} fusion(bf16[512,2048]{1,0:T(8,128)(2,1)} %collective-permute-done.1, bf16[512]{0:T(512)(128)(2,1)S(1)} %fusion.48, bf16[1,8,16,2048]{3,2,1,0:T(8,128)(2,1)S(1)} %copy-done.1, f32[512,8]{0,1:T(8,128)S(1)} %fusion.47), kind=kOutput, calls=%fused_computation.27 | convolution fusion | flops 272752640 | bytes 2671616 | tf_op jit(solution)/shard_map/dot_general | solution.py:79
  58.3 26.9 %all-reduce.6 = (bf16[512,16]{0,1:T(8,128)(2,1)S(1)}, f32[512,16]{0,1:T(8,128)S(1)}, bf16[512,16]{0,1:T(8,128)(2,1)S(1)}) all-reduce(f32[512,16]{0,1:T(8,128)S(1)} %fusion.26, f32[512,16]{0,1:T(8,128)S(1)} %fusion.30, f32[512,16]{0,1:T(8,128)S(1)} %fusion.27), channel_id=1, replica_groups=mesh['section'=4,'tensor'=8,'dp'=8] {'tensor'}, use_global_device_ids=true, to_apply=%region_8.9 | all-reduce | flops 24576 | bytes 163840 | tf_op jit(solution)/shard_map/psum | solution.py:141
  85.3 3.1 %fusion.17 = f32[128,2048]{1,0:T(8,128)} fusion(bf16[512,128]{0,1:T(8,128)(2,1)S(1)} %bitcast.113, bf16[512,2048]{1,0:T(8,128)(2,1)} %collective-permute-done.1, bf16[512]{0:T(512)(128)(2,1)S(1)} %fusion.48), kind=kOutput, calls=%fused_computation.19 | convolution fusion | flops 269484032 | bytes 3277824 | tf_op jit(solution)/shard_map/dot_general | solution.py:85
  88.4 0.0 all-reduce.5.cloned.1.call-update
  88.4 0.4 fusion.8
  88.9 3.8 %fusion.5 = bf16[1,512,2048]{2,1,0:T(8,128)(2,1)} fusion(bf16[512,128]{0,1:T(8,128)(2,1)S(1)} %bitcast.114, bf16[128,2048]{1,0:T(8,128)(2,1)} %bitcast.109, bf16[512,2048]{1,0:T(8,128)(2,1)} %collective-permute-done), kind=kOutput, calls=%fused_computation.9 | convolution fusion | flops 272629760 | bytes 4849664 | tf_op jit(solution)/shard_map/dot_general | solution.py:142
  92.7 60.3 %all-reduce.7 = bf16[128,2048]{1,0:T(8,128)(2,1)} all-reduce(f32[128,2048]{1,0:T(8,128)S(1)} %fusion.8), channel_id=1, replica_groups=mesh['section'=4,'tensor'=8,'dp'=8] {'dp'}, use_global_device_ids=true, to_apply=%region_16.17 | all-reduce | flops 262144 | bytes 1572864 | tf_op jit(solution)/shard_map/psum | solution.py:153
  153.0 19.0 %all-reduce.5.cloned.1.call-done = f32[128,2048]{1,0:T(8,128)} async-done(((f32[128,2048]{1,0:T(8,128)}), f32[128,2048]{1,0:T(8,128)}) %all-reduce.5.cloned.1.call-update) | async-done | bytes 1048592 | tf_op jit(solution)/shard_map/psum | solution.py:153
  172.0 2.1 %multiply_convert_fusion = bf16[128,2048]{1,0:T(8,128)(2,1)} fusion(f32[128,2048]{1,0:T(8,128)} %all-reduce.5.cloned.1.call-done), kind=kLoop, calls=%fused_computation.28 | loop fusion | flops 524288 | bytes 1572864 | tf_op jit(solution)/shard_map/convert_element_type | solution.py:160
  (18 shorter events, 0.1 us)
Async XLA Ops:
  7.2 24.5 %copy-start = (bf16[1,512,2048]{2,1,0:T(8,128)(2,1)S(1)}, bf16[1,512,2048]{2,1,0:T(8,128)(2,1)}, u32[]{:S(2)}) copy-start(bf16[1,512,2048]{2,1,0:T(8,128)(2,1)} %param.15) | copy-start | bytes 6291460
  7.2 10.4 %copy-start.2 = (bf16[1,2,512,128]{3,2,1,0:T(8,128)(2,1)S(1)}, bf16[1,2,512,128]{3,2,1,0:T(8,128)(2,1)}, u32[]{:S(2)}) copy-start(bf16[1,2,512,128]{3,2,1,0:T(8,128)(2,1)} %param.14) | copy-start | bytes 786436
  7.2 164.8 %all-reduce.5.cloned.1.call-start = ((), (), s32[]{:S(2)}) async-start(), calls=%async_computation | async-start | bytes 2097152 | tf_op jit(solution)/shard_map/psum | solution.py:153
  7.2 48.6 %collective-permute-start.1 = (bf16[512,2048]{1,0:T(8,128)(2,1)}, bf16[512,2048]{1,0:T(8,128)(2,1)}, u32[]{:S(2)}, u32[]{:S(2)}) collective-permute-start(bf16[512,2048]{1,0:T(8,128)(2,1)} %bitcast.115), channel_id=1, source_target_pairs={{0,192},{64,0},{128,64},{192,128},{1,193},{65,1},{129,65},{193,129... | collective-permute-start | bytes 6291464 | tf_op jit(solution)/shard_map/ppermute | solution.py:18
  10.6 78.3 %collective-permute-start = (bf16[512,2048]{1,0:T(8,128)(2,1)}, bf16[512,2048]{1,0:T(8,128)(2,1)}, u32[]{:S(2)}, u32[]{:S(2)}) collective-permute-start(bf16[512,2048]{1,0:T(8,128)(2,1)} %bitcast.116), channel_id=1, source_target_pairs={{0,64},{64,128},{128,192},{192,0},{1,65},{65,129},{129,193},{193,1... | collective-permute-start | bytes 6291464 | tf_op jit(solution)/shard_map/ppermute | solution.py:18
  25.5 5.7 %copy-start.3 = (bf16[1,8,16,2048]{3,2,1,0:T(8,128)(2,1)S(1)}, bf16[1,8,16,2048]{3,2,1,0:T(8,128)(2,1)}, u32[]{:S(2)}) copy-start(bf16[1,8,16,2048]{3,2,1,0:T(8,128)(2,1)} %param.16) | copy-start | bytes 1572868
  31.6 24.2 %copy-start.1 = (bf16[1,8,16,2048]{3,2,1,0:T(8,128)(2,1)S(1)}, bf16[1,8,16,2048]{3,2,1,0:T(8,128)(2,1)}, u32[]{:S(2)}) copy-start(bf16[1,8,16,2048]{3,2,1,0:T(8,128)(2,1)} %param.17) | copy-start | bytes 1572868
Sparse Core Ops, SparseCore 0:
  88.5 83.4 all-reduce.4
where the time goes:
time: 184 us; the launch traced here: 181 us
  blocking collectives  87.2 us (47%)
  waiting for transfers between devices  42.3 us (23%)
  matrix products  20.6 us (11%)
  between operations  14.3 us (8%)
  other arithmetic  8.62 us (5%)
  starting transfers between devices  4.34 us (2%)
  local copies, waits for them, and re-layouts  3.57 us (2%)
    psum x1, blocking collectives, per_device(): lax.psum((contract(spread_gradient, saved_rows), contract(spread_rank, ma...  60.3 us
    psum x1, blocking collectives, per_device(): fwd_sum = lax.psum(fwd_part, 'tensor')  26.9 us
    ppermute x2, waiting for transfers between devices, from_behind(): return lax.ppermute(value, axis, pairs)  23.3 us
    psum x1, waiting for transfers between devices, per_device(): lax.psum((contract(spread_gradient, saved_rows), contract(spread_rank, ma...  19 us
    dot_general x1, matrix products, one_block(): jnp.einsum('hgqk,khd->qhgd', weights, value_heads, preferred_element_type...  5.64 us
    ppermute x2, starting transfers between devices, from_behind(): return lax.ppermute(value, axis, pairs)  4.3 us
    reduce_sum x1, other arithmetic, one_block(): row_total = jnp.sum(exponent, axis=-1, keepdims=True)  4.01 us
    dot_general x1, matrix products, one_block(): jnp.einsum('qhgd,khd->hgqk', query_heads, key_heads, preferred_element_ty...  3.87 us
  transfers between devices with their start and end apart: 3, of which 2 were waited for; matrix products, arithmetic and copies ran while one was open for 17% of the time, Pallas kernels for 0%

commit v1 on v0

v1 whole, which is shorter than its diff:
```python
import math

import jax
import jax.numpy as jnp
from jax import lax
from jax.experimental import pallas as pl
from jax.experimental.pallas import tpu as pltpu
from jax.sharding import PartitionSpec as P

HD = 128
BLOCK = 64
SEGS = 3
MOST_BLOCKS = 4
ADAPTER_SCALE = 2.0
BF16 = jnp.bfloat16
F32 = jnp.float32
SMEM = pl.BlockSpec(memory_space=pltpu.SMEM)
VMEM = pl.BlockSpec(memory_space=pltpu.VMEM)
PARAMS = pltpu.CompilerParams(vmem_limit_bytes=48 * 1024 * 1024)


def cost(flops, size, exps=0):
    return pl.CostEstimate(flops=flops, bytes_accessed=size, transcendentals=exps)


def rows_by_rows(left, right):
    return lax.dot_general(left, right, (((1,), (1,)), ((), ())), preferred_element_type=F32)


def segments(blocks, pads, tenants, table, batch):
    starts, lives, slots = [], [], []
    start = jnp.int32(0)
    for i in range(SEGS):
        end = start + blocks[0, batch, 0, i] * BLOCK
        starts.append(start)
        lives.append(end - pads[0, batch, 0, i])
        slots.append(table[tenants[0, batch, 0, i]])
        start = end
    return starts, lives, slots


def alive_rows(starts, lives, first, count):
    token = first + lax.broadcasted_iota(jnp.int32, (1, count), 1)
    return [(token >= s) & (token < e) for s, e in zip(starts, lives)]


def pick_rows(adapters, slots):
    return jnp.concatenate([adapters[0, s] for s in slots], axis=0)


def fold(full, masks, rank):
    return sum(jnp.where(m, full[rank * i : rank * (i + 1)], 0.0) for i, m in enumerate(masks))


def spread(ranked, masks):
    wide = ranked.astype(F32)
    return jnp.concatenate([jnp.where(m, wide, 0.0) for m in masks], axis=0).astype(BF16)


def prepare_kernel(blocks, pads, tenants, table, saved, down, up, out):
    rank, length = up.shape[2], saved.shape[1]
    starts, lives, slots = segments(blocks, pads, tenants, table, 1)
    wide = SEGS * rank
    for i in range(SEGS):
        out[rank * i : rank * (i + 1), :] = up[0, slots[i]]
    masks = alive_rows(starts, lives, 0, length)
    row = lax.broadcasted_iota(jnp.int32, (rank, length), 0)
    notes = jnp.zeros((rank, length), F32)
    for i in range(SEGS):
        notes = jnp.where((row == i) & masks[i], 1.0, notes)
        notes = jnp.where(row == SEGS + i, slots[i].astype(F32), notes)
    back = fold(rows_by_rows(pick_rows(down, slots), saved[0]), masks, rank)
    out[wide:, :length] = notes.astype(BF16)
    out[wide:, length : 2 * length] = back.astype(BF16)
    out[wide:, 2 * length :] = jnp.zeros((rank, out.shape[1] - 2 * length), BF16)


def note_masks(ahead, wide, length):
    notes = ahead[wide:, :length].astype(F32)
    return [notes[i : i + 1] > 0.5 for i in range(SEGS)]


def back_gradient_kernel(ahead, grads, out):
    rank, length = out.shape
    wide = SEGS * rank
    full = rows_by_rows(ahead[:wide, :], grads[0])
    out[...] = fold(full, note_masks(ahead, wide, length), rank).astype(BF16)


def attention_kernel(blocks, pads, tenants, table, queries, keys_values, down, out, attended):
    rank, length = out.shape
    heads = queries.shape[2] // HD
    starts, lives, slots = segments(blocks, pads, tenants, table, 0)
    power = math.log2(math.e) / math.sqrt(HD)
    for j in range(length // BLOCK):
        low, high = max(0, j + 1 - MOST_BLOCKS) * BLOCK, (j + 1) * BLOCK
        here = slice(j * BLOCK, high)
        start, live = starts[0], lives[0]
        for i in range(1, SEGS):
            inside = j * BLOCK >= starts[i]
            start = jnp.where(inside, starts[i], start)
            live = jnp.where(inside, lives[i], live)
        query_at = j * BLOCK + lax.broadcasted_iota(jnp.int32, (BLOCK, high - low), 0)
        key_at = low + lax.broadcasted_iota(jnp.int32, (BLOCK, high - low), 1)
        seen = ((key_at <= query_at) & (key_at >= start))[None]
        alive = (j * BLOCK + lax.broadcasted_iota(jnp.int32, (BLOCK, 1), 0) < live)[None]
        stacked = jnp.concatenate(
            [queries[0, here, HD * h : HD * (h + 1)] for h in range(heads)], axis=0
        )
        scores = rows_by_rows(stacked, keys_values[0, 0, low:high, :])
        scores = jnp.where(seen, scores.reshape(heads, BLOCK, high - low), -1e30)
        top = jnp.max(scores, axis=-1, keepdims=True)
        exponent = jnp.exp2((scores - top) * power)
        total = jnp.sum(exponent, axis=-1, keepdims=True)
        weights = (exponent * jnp.where(alive, 1.0 / total, 0.0)).astype(BF16)
        mixed = jnp.dot(
            weights.reshape(heads * BLOCK, high - low),
            keys_values[0, 1, low:high, :],
            preferred_element_type=F32,
        ).astype(BF16)
        for h in range(heads):
            attended[here, HD * h : HD * (h + 1)] = mixed[BLOCK * h : BLOCK * (h + 1)]
    full = rows_by_rows(pick_rows(down, slots), attended[...])
    out[...] = fold(full, alive_rows(starts, lives, 0, length), rank).astype(BF16)


def contract_kernel(blocks, pads, tenants, table, parts, ahead, saved, grads, fwd, out):
    rank, length = fwd.shape
    wide = SEGS * rank
    starts, lives, slots = segments(blocks, pads, tenants, table, 1)
    total = jnp.sum(parts[...].astype(F32), axis=0)
    fwd[...] = total[:rank].astype(BF16)
    back_rank = total[rank : 2 * rank].astype(BF16)
    back_grad = (ADAPTER_SCALE * total[2 * rank :]).astype(BF16)
    down_part = jnp.dot(
        spread(back_grad, alive_rows(starts, lives, 0, length)), saved[0], preferred_element_type=F32
    ).astype(BF16)
    up_part = jnp.dot(
        spread(back_rank, note_masks(ahead, wide, length)), grads[0], preferred_element_type=F32
    ).astype(BF16)
    count, _, width = out.shape
    row = lax.broadcasted_iota(jnp.int32, (rank, width), 0)
    notes = ahead[wide:, :width].astype(F32)
    for i in range(SEGS):
        notes = jnp.where(row == i, slots[i].astype(F32), notes)
    for d in range(count):
        out[d, :wide, :] = down_part[:, width * d : width * (d + 1)]
        out[d, wide : 2 * wide, :] = up_part[:, width * d : width * (d + 1)]
        out[d, 2 * wide :, :] = notes.astype(BF16)


def collect_kernel(pieces, down_out, up_out):
    count, _, width = pieces.shape
    rows = down_out.shape[0]
    rank = pieces.shape[1] // (2 * SEGS + 1)
    wide = SEGS * rank
    slot_at = lax.broadcasted_iota(jnp.int32, (rows // rank, 1, width), 0).astype(F32)
    for half, ref, scale in ((0, down_out, 1.0), (1, up_out, ADAPTER_SCALE)):
        total = jnp.zeros((rows // rank, rank, width), F32)
        for d in range(count):
            notes = pieces[d, 2 * wide :, :].astype(F32)
            for i in range(SEGS):
                slot = notes[half * SEGS + i : half * SEGS + i + 1]
                first = half * wide + rank * i
                piece = pieces[d, first : first + rank, :].astype(F32)
                total = total + jnp.where(slot_at == slot[None], piece[None], 0.0)
        ref[...] = (scale * total).reshape(rows, width).astype(BF16)


def hand_on_kernel(blocks, pads, tenants, table, arrived, fwd, up, out):
    rows = out.shape[1]
    first = pl.multiple_of(pl.program_id(0) * rows, rows)
    starts, lives, slots = segments(blocks, pads, tenants, table, 0)
    wide = spread(fwd[:, pl.ds(first, rows)], alive_rows(starts, lives, first, rows))
    update = lax.dot_general(
        wide, pick_rows(up, slots), (((0,), (0,)), ((), ())), preferred_element_type=F32
    )
    out[0] = (arrived[0].astype(F32) + ADAPTER_SCALE * update).astype(BF16)


def shift(value, steps):
    count = lax.axis_size("section")
    return lax.ppermute(value, "section", [(i, (i + steps) % count) for i in range(count)])


def per_device(
    act_inbox,
    grad_inbox,
    queries,
    keys_values,
    saved_attn,
    down_adapt,
    up_adapt,
    seg_blocks,
    seg_pads,
    seg_tenant,
    adapter_table,
):
    _, length, width = act_inbox.shape
    _, slot_count, rank, _ = up_adapt.shape
    wide = SEGS * rank
    scalars = (seg_blocks, seg_pads, seg_tenant, adapter_table)
    tensor_count, dp_count = lax.axis_size("tensor"), lax.axis_size("dp")
    part = width // dp_count
    piece = length * width * 2

    ahead = pl.pallas_call(
        prepare_kernel,
        out_shape=jax.ShapeDtypeStruct((wide + rank, width), BF16),
        in_specs=[SMEM] * 4 + [VMEM] * 3,
        out_specs=VMEM,
        compiler_params=PARAMS,
        cost_estimate=cost(2 * wide * length * width, piece * 3 // 2),
        name="prepare",
    )(*scalars, saved_attn, down_adapt, up_adapt)
    ahead = shift(ahead, 1)
    arrived = shift(act_inbox, 1)

    fwd_part = pl.pallas_call(
        attention_kernel,
        out_shape=jax.ShapeDtypeStruct((rank, length), BF16),
        in_specs=[SMEM] * 4 + [VMEM] * 3,
        out_specs=VMEM,
        scratch_shapes=[pltpu.VMEM((length, width), BF16)],
        compiler_params=PARAMS,
        cost_estimate=cost(
            4 * length * MOST_BLOCKS * BLOCK * width + 2 * wide * length * width,
            piece * 3 // 2,
            length * MOST_BLOCKS * BLOCK * width // HD,
        ),
        name="attention",
    )(*scalars, queries, keys_values, down_adapt)

    grad_part = pl.pallas_call(
        back_gradient_kernel,
        out_shape=jax.ShapeDtypeStruct((rank, length), BF16),
        in_specs=[VMEM] * 2,
        out_specs=VMEM,
        compiler_params=PARAMS,
        cost_estimate=cost(2 * wide * length * width, piece),
        name="back_gradient",
    )(ahead, grad_inbox)
    grad_part = shift(grad_part, -1)

    parts = jnp.concatenate([fwd_part, ahead[wide:, length : 2 * length], grad_part], axis=0)
    parts = jnp.broadcast_to(parts[None], (tensor_count, *parts.shape))
    parts = lax.all_to_all(parts, "tensor", 0, 0)

    fwd_rank, pieces = pl.pallas_call(
        contract_kernel,
        out_shape=(
            jax.ShapeDtypeStruct((rank, length), BF16),
            jax.ShapeDtypeStruct((dp_count, 2 * wide + rank, part), BF16),
        ),
        in_specs=[SMEM] * 4 + [VMEM] * 4,
        out_specs=(VMEM, VMEM),
        compiler_params=PARAMS,
        cost_estimate=cost(4 * wide * length * width, 2 * piece),
        name="contract",
    )(*scalars, parts, ahead, saved_attn, grad_inbox)
    pieces = lax.all_to_all(pieces, "dp", 0, 0)

    down_sum, up_sum = pl.pallas_call(
        collect_kernel,
        out_shape=(jax.ShapeDtypeStruct((slot_count * rank, part), BF16),) * 2,
        in_specs=[VMEM],
        out_specs=(VMEM, VMEM),
        compiler_params=PARAMS,
        cost_estimate=cost(4 * dp_count * SEGS * slot_count * rank * part, piece // 4),
        name="collect",
    )(pieces)
    up_sum = shift(up_sum, -1)

    rows = 128
    new_acts = pl.pallas_call(
        hand_on_kernel,
        grid=(length // rows,),
        out_shape=jax.ShapeDtypeStruct(act_inbox.shape, BF16),
        in_specs=[SMEM] * 4 + [pl.BlockSpec((1, rows, width), lambda i: (0, i, 0)), VMEM, VMEM],
        out_specs=pl.BlockSpec((1, rows, width), lambda i: (0, i, 0)),
        compiler_params=PARAMS,
        cost_estimate=cost(2 * wide * length * width, 2 * piece),
        name="hand_on",
    )(*scalars, arrived, fwd_rank, up_adapt)

    sums = jnp.concatenate([down_sum, up_sum], axis=0)
    sums = jnp.broadcast_to(sums[None], (dp_count, *sums.shape))
    sums = lax.all_to_all(sums, "dp", 0, 0)
    sums = sums.transpose(1, 0, 2).reshape(2, 1, slot_count, rank, width)
    return new_acts, sums[0], sums[1]


def solution(mesh):
    placed = (
        P("section", "dp", "tensor"),
        P("section", "dp", "tensor"),
        P("section", "dp", "tensor"),
        P("section", None, "dp", "tensor"),
        P("section", "dp", "tensor"),
        P("section", None, None, "tensor"),
        P("section", None, None, "tensor"),
        P("section", None, "dp", None),
        P("section", None, "dp", None),
        P("section", None, "dp", None),
        P(),
    )
    return jax.shard_map(
        per_device,
        mesh=mesh,
        in_specs=placed,
        out_specs=(
            P("section", "dp", "tensor"),
            P("section", None, None, "tensor"),
            P("section", None, None, "tensor"),
        ),
        check_vma=False,
    )
```

time: 184 us -> 94.1 us (0.51); the launches traced: 181 us -> 93.3 us
  blocking collectives: 87.2 us -> 15.7 us
  matrix products: 20.6 us -> 0 us
  starting transfers between devices: 4.34 us -> 20.9 us
  Pallas kernels: 0 us -> 13.9 us
  between operations: 14.3 us -> 0.83 us
  waiting for transfers between devices: 42.3 us -> 29.4 us
  local copies, waits for them, and re-layouts: 3.57 us -> 12.6 us
  other arithmetic: 8.62 us -> 0.02 us
    psum x2 -> x0, blocking collectives: 87.2 us -> none  [the longest x1 60.3 us: per_device(): lax.psum((contract(spread_gradient, saved_rows), contract(spread_rank, ma...]
    all_to_all x0 -> x2, waiting for transfers between devices: none -> 21.3 us  [the longest x1 12.2 us: per_device(): parts = lax.all_to_all(parts, 'tensor', 0, 0)]
    dot_general x8 -> x0, matrix products: 20.6 us -> none  [the longest x1 5.64 us: one_block(): jnp.einsum('hgqk,khd->qhgd', weights, value_heads, preferred_element_type...]
    psum x1 -> x0, waiting for transfers between devices: 19 us -> none  [per_device(): lax.psum((contract(spread_gradient, saved_rows), contract(spread_rank, ma...]
    all_to_all x0 -> x1, blocking collectives: none -> 15.7 us  [per_device(): pieces = lax.all_to_all(pieces, 'dp', 0, 0)]
    ppermute x2 -> x4, waiting for transfers between devices: 23.3 us -> 8.05 us  [shift(): lax.ppermute(value, 'section', [(i, (i + steps) % count) for i in range(c...]
    pallas_call x0 -> x6, Pallas kernels: none -> 14 us  [the longest x1 5.1 us: per_device(): pl.pallas_call(attention_kernel, out_shape=jax.ShapeDtypeStruct((rank, le...]
    all_to_all x0 -> x2, starting transfers between devices: none -> 10 us  [the longest x1 6.45 us: per_device(): parts = lax.all_to_all(parts, 'tensor', 0, 0)]
  transfers between devices with their start and end apart: 3 -> 6, of which waited for: 2 -> 4; matrix products, arithmetic and copies ran while one was open for 17% -> 1% of each run, Pallas kernels for 0% -> 13%
where the time goes in v1:
time: 94.1 us; the launch traced here: 93.3 us
  waiting for transfers between devices  29.4 us (31%)
  starting transfers between devices  20.9 us (22%)
  blocking collectives  15.7 us (17%)
  Pallas kernels  13.9 us (15%)
  local copies, waits for them, and re-layouts  12.6 us (13%)
    all_to_all x1, blocking collectives, per_device(): pieces = lax.all_to_all(pieces, 'dp', 0, 0)  15.7 us
    all_to_all x1, waiting for transfers between devices, per_device(): parts = lax.all_to_all(parts, 'tensor', 0, 0)  12.2 us
    ppermute x4, starting transfers between devices, shift(): lax.ppermute(value, 'section', [(i, (i + steps) % count) for i in range(c...  10.9 us
    all_to_all x1, waiting for transfers between devices, per_device(): sums = lax.all_to_all(sums, 'dp', 0, 0)  9.09 us
    ppermute x4, waiting for transfers between devices, shift(): lax.ppermute(value, 'section', [(i, (i + steps) % count) for i in range(c...  8.05 us
    unnamed x36, local copies, waits for them, and re-layouts  7.99 us
    all_to_all x1, starting transfers between devices, per_device(): parts = lax.all_to_all(parts, 'tensor', 0, 0)  6.45 us
    pallas_call x1, Pallas kernels, per_device(): pl.pallas_call(attention_kernel, out_shape=jax.ShapeDtypeStruct((rank, le...  5.1 us
  transfers between devices with their start and end apart: 6, of which 4 were waited for; matrix products, arithmetic and copies ran while one was open for 1% of the time, Pallas kernels for 13%

profile of v1, /device:TPU:1, one launch (start us, length us, event | category | flops | bytes accessed | tf_op | source)
XLA Modules:
  0.0 93.3 jit_solution(13345692726827381778)
XLA Ops:
  0.6 1.6 %copy-done = bf16[1,512,2048]{2,1,0:T(8,128)(2,1)S(1)} copy-done((bf16[1,512,2048]{2,1,0:T(8,128)(2,1)S(1)}, bf16[1,512,2048]{2,1,0:T(8,128)(2,1)}, u32[]{:S(2)}) %copy-start) | copy-done | bytes 2097176
  2.2 1.0 %copy-done.4 = bf16[1,8,16,2048]{3,2,1,0:T(8,128)(2,1)S(1)} copy-done((bf16[1,8,16,2048]{3,2,1,0:T(8,128)(2,1)S(1)}, bf16[1,8,16,2048]{3,2,1,0:T(8,128)(2,1)}, u32[]{:S(2)}) %copy-start.4) | copy-done | bytes 524312
  3.3 1.0 %copy-done.6 = bf16[1,8,16,2048]{3,2,1,0:T(8,128)(2,1)S(1)} copy-done((bf16[1,8,16,2048]{3,2,1,0:T(8,128)(2,1)S(1)}, bf16[1,8,16,2048]{3,2,1,0:T(8,128)(2,1)}, u32[]{:S(2)}) %copy-start.6) | copy-done | bytes 524312
  4.3 0.7 copy-done.8
  5.0 0.7 copy-done.10
  5.7 0.7 copy-done.12
  6.3 0.7 copy-done.14
  7.0 1.3 %prepare.1 = bf16[64,2048]{1,0:T(8,128)(2,1)S(1)} custom-call(s32[1,2,1,3]{3,2,1,0:T(1,128)S(1)} %copy-done.8, s32[1,2,1,3]{3,2,1,0:T(1,128)S(1)} %copy-done.10, s32[1,2,1,3]{3,2,1,0:T(1,128)S(1)} %copy-done.12, s32[32]{0:T(128)S(1)} %copy-done.14, bf16[1,512,2048]{2,1,0:T(8,128)(2,1)S(1)} %copy-done, bf16[1,8,16,2048]{3,2,1,0:T(8,128)(2,1)S(1)} %copy-done.6, ...), custom_call_target="tpu_custom_call" | custom-call | flops 100663296 | bytes 3145728 | tf_op jit(solution)/shard_map/prepare/pallas_call | solution.py:207
  8.3 4.2 %collective-permute-start.1 = (bf16[64,2048]{1,0:T(8,128)(2,1)S(1)}, bf16[64,2048]{1,0:T(8,128)(2,1)S(1)}, u32[]{:S(2)}, u32[]{:S(2)}) collective-permute-start(bf16[64,2048]{1,0:T(8,128)(2,1)S(1)} %prepare.1), channel_id=1, source_target_pairs={{0,64},{64,128},{128,192},{192,0},{1,65},{65,129},{129,193},{193,1... | collective-permute-start | bytes 786440 | tf_op jit(solution)/shard_map/ppermute | solution.py:183
  12.6 3.3 %collective-permute-done.1.ahead = bf16[64,2048]{1,0:T(8,128)(2,1)S(1)} collective-permute-done((bf16[64,2048]{1,0:T(8,128)(2,1)S(1)}, bf16[64,2048]{1,0:T(8,128)(2,1)S(1)}, u32[]{:S(2)}, u32[]{:S(2)}) %collective-permute-start.1) | collective-permute-done | bytes 262176 | tf_op jit(solution)/shard_map/ppermute | solution.py:183
  15.9 0.7 back_gradient.1
  16.7 3.2 %collective-permute-start.2 = (bf16[16,512]{1,0:T(8,128)(2,1)S(1)}, bf16[16,512]{1,0:T(8,128)(2,1)S(1)}, u32[]{:S(2)}, u32[]{:S(2)}) collective-permute-start(bf16[16,512]{1,0:T(8,128)(2,1)S(1)} %back_gradient.1), channel_id=1, source_target_pairs={{0,192},{64,0},{128,64},{192,128},{1,193},{65,1},{129,65},{193,129... | collective-permute-start | bytes 49160 | tf_op jit(solution)/shard_map/ppermute | solution.py:183
  19.9 5.1 %attention.1 = bf16[16,512]{1,0:T(8,128)(2,1)S(1)} custom-call(s32[1,2,1,3]{3,2,1,0:T(1,128)S(1)} %copy-done.8, s32[1,2,1,3]{3,2,1,0:T(1,128)S(1)} %copy-done.10, s32[1,2,1,3]{3,2,1,0:T(1,128)S(1)} %copy-done.12, s32[32]{0:T(128)S(1)} %copy-done.14, bf16[1,512,2048]{2,1,0:T(8,128)(2,1)S(1)} %copy-done.16, bf16[1,2,512,128]{3,2,1,0:T(8,128)(2,1)S(1)} %copy-done.17, ...), custom_call_target="tpu_custom_call" | custom-call | flops 1174405120 | bytes 3145728 | tf_op jit(solution)/shard_map/attention/pallas_call | solution.py:219
  25.0 0.8 broadcast_in_dim.4
  25.8 6.5 %all-to-all-start = ((bf16[8,48,512]{2,1,0:T(8,128)(2,1)}), bf16[8,48,512]{2,1,0:T(8,128)(2,1)S(1)}, u32[]{:S(2)}, u32[]{:S(2)}) async-start(bf16[8,48,512]{2,1,0:T(8,128)(2,1)} %broadcast_in_dim.4), calls=%async_computation | async-start | bytes 786432 | tf_op jit(solution)/shard_map/all_to_all | solution.py:247
  32.2 2.9 %collective-permute-start = (bf16[1,512,2048]{2,1,0:T(8,128)(2,1)}, bf16[1,512,2048]{2,1,0:T(8,128)(2,1)}, u32[]{:S(2)}, u32[]{:S(2)}) collective-permute-start(bf16[1,512,2048]{2,1,0:T(8,128)(2,1)} %param.11), channel_id=1, source_target_pairs={{0,64},{64,128},{128,192},{192,0},{1,65},{65,129},{129,193},{193,1... | collective-permute-start | bytes 6291464 | tf_op jit(solution)/shard_map/ppermute | solution.py:183
  35.2 12.2 %all-to-all-done.parts = bf16[8,48,512]{2,1,0:T(8,128)(2,1)S(1)} async-done(((bf16[8,48,512]{2,1,0:T(8,128)(2,1)}), bf16[8,48,512]{2,1,0:T(8,128)(2,1)S(1)}, u32[]{:S(2)}, u32[]{:S(2)}) %all-to-all-start) | async-done | bytes 393248 | tf_op jit(solution)/shard_map/all_to_all | solution.py:247
  47.5 1.6 %copy-done.3 = bf16[1,512,2048]{2,1,0:T(8,128)(2,1)S(1)} copy-done((bf16[1,512,2048]{2,1,0:T(8,128)(2,1)S(1)}, bf16[1,512,2048]{2,1,0:T(8,128)(2,1)}, u32[]{:S(2)}) %copy-start.3) | copy-done | bytes 2097176
  49.0 1.4 %contract.1 = (bf16[16,512]{1,0:T(8,128)(2,1)S(1)}, bf16[8,112,256]{2,1,0:T(8,128)(2,1)S(1)}) custom-call(s32[1,2,1,3]{3,2,1,0:T(1,128)S(1)} %copy-done.9, s32[1,2,1,3]{3,2,1,0:T(1,128)S(1)} %copy-done.11, s32[1,2,1,3]{3,2,1,0:T(1,128)S(1)} %copy-done.13, s32[32]{0:T(128)S(1)} %copy-done.15, bf16[8,48,512]{2,1,0:T(8,128)(2,1)S(1)} %all-to-all-done.parts, ...), custom_call_target="tpu_custom_call" | custom-call | flops 201326592 | bytes 4194304 | tf_op jit(solution)/shard_map/contract/pallas_call | solution.py:249
  50.5 15.7 %all_to_all.15.pieces = bf16[8,112,256]{2,1,0:T(8,128)(2,1)S(1)} all-to-all(bf16[8,112,256]{2,1,0:T(8,128)(2,1)S(1)} %get-tuple-element.8), channel_id=1, replica_groups=mesh['section'=4,'tensor'=8,'dp'=8] {'dp'}, dimensions={0} | all-to-all | bytes 917504 | tf_op jit(solution)/shard_map/all_to_all | solution.py:261
  66.2 1.0 %collect.1 = (bf16[128,256]{1,0:T(8,128)(2,1)S(1)}, bf16[128,256]{1,0:T(8,128)(2,1)S(1)}) custom-call(bf16[8,112,256]{2,1,0:T(8,128)(2,1)S(1)} %all_to_all.15.pieces), custom_call_target="tpu_custom_call" | custom-call | flops 3145728 | bytes 524288 | tf_op jit(solution)/shard_map/collect/pallas_call | solution.py:263
  67.1 0.5 collective-permute-start.3
  67.7 4.7 %collective-permute-done.3 = bf16[128,256]{1,0:T(8,128)(2,1)S(1)} collective-permute-done((bf16[128,256]{1,0:T(8,128)(2,1)S(1)}, bf16[128,256]{1,0:T(8,128)(2,1)S(1)}, u32[]{:S(2)}, u32[]{:S(2)}) %collective-permute-start.3) | collective-permute-done | bytes 65568 | tf_op jit(solution)/shard_map/ppermute | solution.py:183
  72.4 1.1 %broadcast_in_dim.5 = bf16[8,256,256]{2,1,0:T(8,128)(2,1)} broadcast(bf16[256,256]{1,0:T(8,128)(2,1)S(1)} %pad_maximum_fusion), dimensions={1,2} | broadcast | bytes 1179648 | tf_op jit(solution)/shard_map/broadcast_in_dim | solution.py:287
  73.5 3.6 %all-to-all-start.2 = ((bf16[8,256,256]{2,1,0:T(8,128)(2,1)}), bf16[8,256,256]{2,1,0:T(8,128)(2,1)S(1)}, u32[]{:S(2)}, u32[]{:S(2)}) async-start(bf16[8,256,256]{2,1,0:T(8,128)(2,1)} %broadcast_in_dim.5), calls=%async_computation.2 | async-start | bytes 2097152 | tf_op jit(solution)/shard_map/all_to_all | solution.py:288
  77.1 4.4 %hand_on.1 = bf16[1,512,2048]{2,1,0:T(8,128)(2,1)} custom-call(s32[1,2,1,3]{3,2,1,0:T(1,128)S(1)} %copy-done.9, s32[1,2,1,3]{3,2,1,0:T(1,128)S(1)} %copy-done.11, s32[1,2,1,3]{3,2,1,0:T(1,128)S(1)} %copy-done.13, s32[32]{0:T(128)S(1)} %copy-done.15, bf16[1,512,2048]{2,1,0:T(8,128)(2,1)} %collective-permute-done.arrived, ...), custom_call_target="tpu_custom_call" | custom-call | flops 100663296 | bytes 4194304 | tf_op jit(solution)/shard_map/hand_on/pallas_call | solution.py:275
  81.5 9.1 %all-to-all-done.2 = bf16[8,256,256]{2,1,0:T(8,128)(2,1)S(1)} async-done(((bf16[8,256,256]{2,1,0:T(8,128)(2,1)}), bf16[8,256,256]{2,1,0:T(8,128)(2,1)S(1)}, u32[]{:S(2)}, u32[]{:S(2)}) %all-to-all-start.2) | async-done | bytes 1048608 | tf_op jit(solution)/shard_map/all_to_all | solution.py:288
  90.6 0.1 fusion
  90.6 0.3 copy.14
  90.9 1.0 %squeeze.6 = bf16[1,8,16,2048]{3,2,1,0:T(8,128)(2,1)} reshape(bf16[128,8,256]{2,1,0:T(8,128)(2,1)S(1)} %copy.14) | data formatting | bytes 1048576 | tf_op jit(solution)/shard_map/squeeze | solution.py:290
  92.0 0.3 copy.15
  92.3 1.0 %squeeze.7 = bf16[1,8,16,2048]{3,2,1,0:T(8,128)(2,1)} reshape(bf16[128,8,256]{2,1,0:T(8,128)(2,1)S(1)} %copy.15) | data formatting | bytes 1048576 | tf_op jit(solution)/shard_map/squeeze | solution.py:290
  (33 shorter events, 0.1 us)
Async XLA Ops:
  0.6 1.6 %copy-start = (bf16[1,512,2048]{2,1,0:T(8,128)(2,1)S(1)}, bf16[1,512,2048]{2,1,0:T(8,128)(2,1)}, u32[]{:S(2)}) copy-start(bf16[1,512,2048]{2,1,0:T(8,128)(2,1)} %saved.3) | copy-start | bytes 6291460
  2.2 1.0 %copy-start.4 = (bf16[1,8,16,2048]{3,2,1,0:T(8,128)(2,1)S(1)}, bf16[1,8,16,2048]{3,2,1,0:T(8,128)(2,1)}, u32[]{:S(2)}) copy-start(bf16[1,8,16,2048]{3,2,1,0:T(8,128)(2,1)} %up.3) | copy-start | bytes 1572868
  3.3 1.0 %copy-start.6 = (bf16[1,8,16,2048]{3,2,1,0:T(8,128)(2,1)S(1)}, bf16[1,8,16,2048]{3,2,1,0:T(8,128)(2,1)}, u32[]{:S(2)}) copy-start(bf16[1,8,16,2048]{3,2,1,0:T(8,128)(2,1)} %down.3) | copy-start | bytes 1572868
  4.3 0.7 copy-start.8
  5.0 0.7 copy-start.10
  5.7 0.7 copy-start.12
  6.3 0.7 copy-start.14
  7.0 8.9 %copy-start.2 = (bf16[1,512,2048]{2,1,0:T(8,128)(2,1)S(1)}, bf16[1,512,2048]{2,1,0:T(8,128)(2,1)}, u32[]{:S(2)}) copy-start(bf16[1,512,2048]{2,1,0:T(8,128)(2,1)} %grads.3) | copy-start | bytes 6291460
  7.0 12.9 %copy-start.7 = (bf16[1,8,16,2048]{3,2,1,0:T(8,128)(2,1)S(1)}, bf16[1,8,16,2048]{3,2,1,0:T(8,128)(2,1)}, u32[]{:S(2)}) copy-start(bf16[1,8,16,2048]{3,2,1,0:T(8,128)(2,1)} %down.3) | copy-start | bytes 1572868
  7.0 12.9 %copy-start.16 = (bf16[1,512,2048]{2,1,0:T(8,128)(2,1)S(1)}, bf16[1,512,2048]{2,1,0:T(8,128)(2,1)}, u32[]{:S(2)}) copy-start(bf16[1,512,2048]{2,1,0:T(8,128)(2,1)} %queries.1) | copy-start | bytes 6291460
  7.0 12.9 %copy-start.17 = (bf16[1,2,512,128]{3,2,1,0:T(8,128)(2,1)S(1)}, bf16[1,2,512,128]{3,2,1,0:T(8,128)(2,1)}, u32[]{:S(2)}) copy-start(bf16[1,2,512,128]{3,2,1,0:T(8,128)(2,1)} %keys_values.1) | copy-start | bytes 786436
  8.3 7.5 %collective-permute-start.1 = (bf16[64,2048]{1,0:T(8,128)(2,1)S(1)}, bf16[64,2048]{1,0:T(8,128)(2,1)S(1)}, u32[]{:S(2)}, u32[]{:S(2)}) collective-permute-start(bf16[64,2048]{1,0:T(8,128)(2,1)S(1)} %prepare.1), channel_id=1, source_target_pairs={{0,64},{64,128},{128,192},{192,0},{1,65},{65,129},{129,193},{193,1... | collective-permute-start | bytes 786440 | tf_op jit(solution)/shard_map/ppermute | solution.py:183
  16.6 30.8 %copy-start.1 = (bf16[1,512,2048]{2,1,0:T(8,128)(2,1)S(1)}, bf16[1,512,2048]{2,1,0:T(8,128)(2,1)}, u32[]{:S(2)}) copy-start(bf16[1,512,2048]{2,1,0:T(8,128)(2,1)} %saved.3) | copy-start | bytes 6291460
  16.6 30.8 %copy-start.9 = (s32[1,2,1,3]{3,2,1,0:T(1,128)S(1)}, s32[1,2,1,3]{3,2,1,0:T(1,128)}, u32[]{:S(2)}) copy-start(s32[1,2,1,3]{3,2,1,0:T(1,128)} %blocks.7) | copy-start | bytes 76
  16.7 30.8 %copy-start.11 = (s32[1,2,1,3]{3,2,1,0:T(1,128)S(1)}, s32[1,2,1,3]{3,2,1,0:T(1,128)}, u32[]{:S(2)}) copy-start(s32[1,2,1,3]{3,2,1,0:T(1,128)} %pads.7) | copy-start | bytes 76
  16.7 30.8 %copy-start.13 = (s32[1,2,1,3]{3,2,1,0:T(1,128)S(1)}, s32[1,2,1,3]{3,2,1,0:T(1,128)}, u32[]{:S(2)}) copy-start(s32[1,2,1,3]{3,2,1,0:T(1,128)} %tenants.7) | copy-start | bytes 76
  16.7 30.8 %copy-start.15 = (s32[32]{0:T(128)S(1)}, s32[32]{0:T(128)}, u32[]{:S(2)}) copy-start(s32[32]{0:T(128)} %table.7) | copy-start | bytes 388
  16.7 8.3 %collective-permute-start.2 = (bf16[16,512]{1,0:T(8,128)(2,1)S(1)}, bf16[16,512]{1,0:T(8,128)(2,1)S(1)}, u32[]{:S(2)}, u32[]{:S(2)}) collective-permute-start(bf16[16,512]{1,0:T(8,128)(2,1)S(1)} %back_gradient.1), channel_id=1, source_target_pairs={{0,192},{64,0},{128,64},{192,128},{1,193},{65,1},{129,65},{193,129... | collective-permute-start | bytes 49160 | tf_op jit(solution)/shard_map/ppermute | solution.py:183
  25.8 21.6 %all-to-all-start = ((bf16[8,48,512]{2,1,0:T(8,128)(2,1)}), bf16[8,48,512]{2,1,0:T(8,128)(2,1)S(1)}, u32[]{:S(2)}, u32[]{:S(2)}) async-start(bf16[8,48,512]{2,1,0:T(8,128)(2,1)} %broadcast_in_dim.4), calls=%async_computation | async-start | bytes 786432 | tf_op jit(solution)/shard_map/all_to_all | solution.py:247
  32.2 44.8 %collective-permute-start = (bf16[1,512,2048]{2,1,0:T(8,128)(2,1)}, bf16[1,512,2048]{2,1,0:T(8,128)(2,1)}, u32[]{:S(2)}, u32[]{:S(2)}) collective-permute-start(bf16[1,512,2048]{2,1,0:T(8,128)(2,1)} %param.11), channel_id=1, source_target_pairs={{0,64},{64,128},{128,192},{192,0},{1,65},{65,129},{129,193},{193,1... | collective-permute-start | bytes 6291464 | tf_op jit(solution)/shard_map/ppermute | solution.py:183
  47.4 1.6 %copy-start.3 = (bf16[1,512,2048]{2,1,0:T(8,128)(2,1)S(1)}, bf16[1,512,2048]{2,1,0:T(8,128)(2,1)}, u32[]{:S(2)}) copy-start(bf16[1,512,2048]{2,1,0:T(8,128)(2,1)} %grads.3) | copy-start | bytes 6291460
  66.2 10.9 %copy-start.5 = (bf16[1,8,16,2048]{3,2,1,0:T(8,128)(2,1)S(1)}, bf16[1,8,16,2048]{3,2,1,0:T(8,128)(2,1)}, u32[]{:S(2)}) copy-start(bf16[1,8,16,2048]{3,2,1,0:T(8,128)(2,1)} %up.3) | copy-start | bytes 1572868
  67.1 5.3 %collective-permute-start.3 = (bf16[128,256]{1,0:T(8,128)(2,1)S(1)}, bf16[128,256]{1,0:T(8,128)(2,1)S(1)}, u32[]{:S(2)}, u32[]{:S(2)}) collective-permute-start(bf16[128,256]{1,0:T(8,128)(2,1)S(1)} %get-tuple-element.10), channel_id=1, source_target_pairs={{0,192},{64,0},{128,64},{192,128},{1,193},{65,1},{129,65},{193,129... | collective-permute-start | bytes 196616 | tf_op jit(solution)/shard_map/ppermute | solution.py:183
  73.5 17.1 %all-to-all-start.2 = ((bf16[8,256,256]{2,1,0:T(8,128)(2,1)}), bf16[8,256,256]{2,1,0:T(8,128)(2,1)S(1)}, u32[]{:S(2)}, u32[]{:S(2)}) async-start(bf16[8,256,256]{2,1,0:T(8,128)(2,1)} %broadcast_in_dim.5), calls=%async_computation.2 | async-start | bytes 2097152 | tf_op jit(solution)/shard_map/all_to_all | solution.py:288

commit v2 on v1

v2 whole, which is shorter than its diff:
```python
import math

import jax
import jax.numpy as jnp
from jax import lax
from jax.experimental import pallas as pl
from jax.experimental.pallas import tpu as pltpu
from jax.sharding import PartitionSpec as P

HD = 128
BLOCK = 64
SEGS = 3
MOST_BLOCKS = 4
ADAPTER_SCALE = 2.0
BF16 = jnp.bfloat16
F32 = jnp.float32
SMEM = pl.BlockSpec(memory_space=pltpu.SMEM)
VMEM = pl.BlockSpec(memory_space=pltpu.VMEM)
HBM = pl.BlockSpec(memory_space=pltpu.HBM)
PARAMS = pltpu.CompilerParams(vmem_limit_bytes=20 * 1024 * 1024)


def cost(flops, size, exps=0):
    return pl.CostEstimate(flops=flops, bytes_accessed=size, transcendentals=exps)


def rows_by_rows(left, right):
    return lax.dot_general(left, right, (((1,), (1,)), ((), ())), preferred_element_type=F32)


def segments(blocks, pads, tenants, table, batch):
    starts, lives, slots = [], [], []
    start = jnp.int32(0)
    for i in range(SEGS):
        end = start + blocks[0, batch, 0, i] * BLOCK
        starts.append(start)
        lives.append(end - pads[0, batch, 0, i])
        slots.append(table[tenants[0, batch, 0, i]])
        start = end
    return starts, lives, slots


def alive_rows(starts, lives, first, count):
    token = first + lax.broadcasted_iota(jnp.int32, (1, count), 1)
    return [(token >= s) & (token < e) for s, e in zip(starts, lives)]


def pick_rows(adapters, slots):
    return jnp.concatenate([adapters[0, s] for s in slots], axis=0)


def fold(full, masks, rank):
    return sum(jnp.where(m, full[rank * i : rank * (i + 1)], 0.0) for i, m in enumerate(masks))


def spread(ranked, masks):
    wide = ranked.astype(F32)
    return jnp.concatenate([jnp.where(m, wide, 0.0) for m in masks], axis=0).astype(BF16)


def prepare_kernel(blocks, pads, tenants, table, saved, down, up, out, info, raw, listed, held, downs, ups, sems):
    _, _, rank, width = up.shape
    length = saved.shape[1]
    wide = SEGS * rank
    cuts = sems.shape[0] - 6
    tall = length // cuts
    first = [pltpu.make_async_copy(src, raw.at[i], sems.at[i]) for i, src in enumerate((blocks, pads, tenants))]
    first.append(pltpu.make_async_copy(table, listed, sems.at[3]))
    adapters = [
        pltpu.make_async_copy(up, ups, sems.at[4]),
        pltpu.make_async_copy(down, downs, sems.at[5]),
    ]
    later = []
    for i in range(cuts):
        at = pl.ds(tall * i, tall)
        later.append(pltpu.make_async_copy(saved.at[0, at], held.at[at], sems.at[6 + i]))
    for copy in first + later + adapters:
        copy.start()
    for copy in first:
        copy.wait()
    for batch in range(2):
        found = segments(raw.at[0], raw.at[1], raw.at[2], listed, batch)
        for i, values in enumerate(found):
            for k, value in enumerate(values):
                info[0, SEGS * (SEGS * batch + i) + k] = value
    starts, lives, slots = found
    masks = alive_rows(starts, lives, 0, length)
    row = lax.broadcasted_iota(jnp.int32, (rank, length), 0)
    notes = jnp.zeros((rank, length), F32)
    for i in range(SEGS):
        notes = jnp.where((row == i) & masks[i], 1.0, notes)
        notes = jnp.where(row == SEGS + i, slots[i].astype(F32), notes)
    out[wide:, :length] = notes.astype(BF16)
    out[wide:, 2 * length :] = jnp.zeros((rank, width - 2 * length), BF16)
    adapters[0].wait()
    for i in range(SEGS):
        out[rank * i : rank * (i + 1), :] = ups[0, slots[i]]
    adapters[1].wait()
    rows = pick_rows(downs, slots)
    for i, copy in enumerate(later):
        copy.wait()
        at = slice(tall * i, tall * (i + 1))
        back = fold(rows_by_rows(rows, held[at]), [m[:, at] for m in masks], rank)
        out[wide:, length + tall * i : length + tall * (i + 1)] = back.astype(BF16)


def recall(info, batch):
    base = SEGS * SEGS * batch
    return [[info[0, base + SEGS * i + k] for k in range(SEGS)] for i in range(3)]


def note_masks(ahead, wide, length):
    notes = ahead[wide:, :length].astype(F32)
    return [notes[i : i + 1] > 0.5 for i in range(SEGS)]


def back_gradient_kernel(ahead, grads, out):
    rank, length = out.shape
    wide = SEGS * rank
    full = rows_by_rows(ahead[:wide, :], grads[0])
    out[...] = fold(full, note_masks(ahead, wide, length), rank).astype(BF16)


def attend_blocks(info, queries, keys_values, attended, first, last, base):
    heads = queries.shape[2] // HD
    starts, lives, _ = recall(info, 0)
    power = math.log2(math.e) / math.sqrt(HD)
    for j in range(first, last):
        low, high = max(0, j + 1 - MOST_BLOCKS) * BLOCK, (j + 1) * BLOCK
        here = slice(j * BLOCK, high)
        start, live = starts[0], lives[0]
        for i in range(1, SEGS):
            inside = j * BLOCK >= starts[i]
            start = jnp.where(inside, starts[i], start)
            live = jnp.where(inside, lives[i], live)
        query_at = j * BLOCK + lax.broadcasted_iota(jnp.int32, (BLOCK, high - low), 0)
        key_at = low + lax.broadcasted_iota(jnp.int32, (BLOCK, high - low), 1)
        seen = ((key_at <= query_at) & (key_at >= start))[None]
        alive = (j * BLOCK + lax.broadcasted_iota(jnp.int32, (BLOCK, 1), 0) < live)[None]
        stacked = jnp.concatenate(
            [queries[0, here, HD * h : HD * (h + 1)] for h in range(heads)], axis=0
        )
        scores = rows_by_rows(stacked, keys_values[0, 0, low:high, :])
        scores = jnp.where(seen, scores.reshape(heads, BLOCK, high - low), -1e30)
        top = jnp.max(scores, axis=-1, keepdims=True)
        exponent = jnp.exp2((scores - top) * power)
        total = jnp.sum(exponent, axis=-1, keepdims=True)
        weights = (exponent * jnp.where(alive, 1.0 / total, 0.0)).astype(BF16)
        mixed = jnp.dot(
            weights.reshape(heads * BLOCK, high - low),
            keys_values[0, 1, low:high, :],
            preferred_element_type=F32,
        ).astype(BF16)
        for h in range(heads):
            at = slice((j - base) * BLOCK, (j + 1 - base) * BLOCK)
            attended[at, HD * h : HD * (h + 1)] = mixed[BLOCK * h : BLOCK * (h + 1)]


def ranked_attention(info, down, attended, first, out):
    rank, length = out.shape
    starts, lives, slots = recall(info, 0)
    full = rows_by_rows(pick_rows(down, slots), attended[...])
    out[...] = fold(full, alive_rows(starts, lives, first, length), rank)


def early_attention_kernel(info, queries, keys_values, down, out, attended):
    attend_blocks(info, queries, keys_values, attended, 0, attended.shape[0] // BLOCK, 0)
    ranked_attention(info, down, attended, 0, out)


def late_attention_kernel(info, queries, keys_values, down, out, attended):
    half = attended.shape[0] // BLOCK
    attend_blocks(info, queries, keys_values, attended, half, 2 * half, half)
    ranked_attention(info, down, attended, half * BLOCK, out)


def contract_kernel(info, parts, ahead, saved, grads, out, held, sems):
    _, rows, length = parts.shape
    rank = rows // 2
    wide = SEGS * rank
    cuts = sems.shape[1]
    tall = length // cuts
    copies = []
    for k, ref in enumerate((saved, grads)):
        for i in range(cuts):
            at = pl.ds(tall * i, tall)
            copies.append(pltpu.make_async_copy(ref.at[0, at], held.at[k, at], sems.at[k, i]))
    for copy in copies:
        copy.start()
    starts, lives, slots = recall(info, 1)
    total = jnp.sum(parts[...].astype(F32), axis=0)
    back_rank = total[:rank].astype(BF16)
    back_grad = (ADAPTER_SCALE * total[rank:]).astype(BF16)
    count, _, width = out.shape
    row = lax.broadcasted_iota(jnp.int32, (rank, width), 0)
    notes = ahead[wide:, :width].astype(F32)
    for i in range(SEGS):
        notes = jnp.where(row == i, slots[i].astype(F32), notes)
    lefts = (
        spread(back_grad, alive_rows(starts, lives, 0, length)),
        spread(back_rank, note_masks(ahead, wide, length)),
    )
    for d in range(count):
        out[d, 2 * wide :, :] = notes.astype(BF16)
    for k, left in enumerate(lefts):
        for copy in copies[cuts * k : cuts * (k + 1)]:
            copy.wait()
        full = jnp.dot(left, held[k], preferred_element_type=F32).astype(BF16)
        for d in range(count):
            out[d, wide * k : wide * (k + 1), :] = full[:, width * d : width * (d + 1)]


def collect(pieces, half, scale, rows):
    count, _, width = pieces.shape
    rank = pieces.shape[1] // (2 * SEGS + 1)
    wide = SEGS * rank
    slot_at = lax.broadcasted_iota(jnp.int32, (rows // rank, 1, width), 0).astype(F32)
    total = jnp.zeros((rows // rank, rank, width), F32)
    for d in range(count):
        notes = pieces[d, 2 * wide :, :].astype(F32)
        for i in range(SEGS):
            slot = notes[half * SEGS + i : half * SEGS + i + 1]
            first = half * wide + rank * i
            piece = pieces[d, first : first + rank, :].astype(F32)
            total = total + jnp.where(slot_at == slot[None], piece[None], 0.0)
    return (scale * total).reshape(rows, width).astype(BF16)


def collect_kernel(pieces, down_out, up_out):
    down_out[...] = collect(pieces, 0, 1.0, down_out.shape[0])
    up_out[...] = collect(pieces, 1, ADAPTER_SCALE, up_out.shape[0])


def unpack_kernel(sums, down_out, up_out):
    count, rows, width = sums.shape
    for half, ref in enumerate((down_out, up_out)):
        _, slots, rank, _ = ref.shape
        for d in range(count):
            block = sums[d, half * (rows // 2) : (half + 1) * (rows // 2)]
            ref[0, :, :, width * d : width * (d + 1)] = block.reshape(slots, rank, width)


def hand_on_kernel(info, arrived, fwd, up, out):
    rows = out.shape[1]
    first = pl.multiple_of(pl.program_id(0) * rows, rows)
    starts, lives, slots = recall(info, 0)
    wide = spread(fwd[:, pl.ds(first, rows)], alive_rows(starts, lives, first, rows))
    update = lax.dot_general(
        wide, pick_rows(up, slots), (((0,), (0,)), ((), ())), preferred_element_type=F32
    )
    out[0] = (arrived[0].astype(F32) + ADAPTER_SCALE * update).astype(BF16)


def in_hbm(value):
    return pltpu.with_memory_space_constraint(value, pltpu.HBM)


def shift(value, steps):
    count = lax.axis_size("section")
    return lax.ppermute(value, "section", [(i, (i + steps) % count) for i in range(count)])


def exchange_add(value, distance):
    count = lax.axis_size("tensor")
    return value + lax.ppermute(value, "tensor", [(i, i ^ distance) for i in range(count)])


def per_device(
    act_inbox,
    grad_inbox,
    queries,
    keys_values,
    saved_attn,
    down_adapt,
    up_adapt,
    seg_blocks,
    seg_pads,
    seg_tenant,
    adapter_table,
):
    _, length, width = act_inbox.shape
    _, slot_count, rank, _ = up_adapt.shape
    wide = SEGS * rank
    scalars = (seg_blocks, seg_pads, seg_tenant, adapter_table)
    tensor_count, dp_count = lax.axis_size("tensor"), lax.axis_size("dp")
    part = width // dp_count
    piece = length * width * 2

    cuts = 1
    vmem = lambda shape: pltpu.VMEM(shape, BF16)
    ahead, info = pl.pallas_call(
        prepare_kernel,
        out_shape=(vmem((wide + rank, width)), jax.ShapeDtypeStruct((1, 2 * SEGS * SEGS), jnp.int32)),
        in_specs=[HBM] * 7,
        out_specs=(VMEM, SMEM),
        scratch_shapes=[
            pltpu.SMEM((3, *seg_blocks.shape), jnp.int32),
            pltpu.SMEM(adapter_table.shape, jnp.int32),
            pltpu.VMEM((length, width), BF16),
            pltpu.VMEM(down_adapt.shape, BF16),
            pltpu.VMEM(up_adapt.shape, BF16),
            pltpu.SemaphoreType.DMA((6 + cuts,)),
        ],
        compiler_params=PARAMS,
        cost_estimate=cost(2 * wide * length * width, 5 * piece),
        name="prepare",
    )(*[in_hbm(x) for x in (*scalars, saved_attn, down_adapt, up_adapt)])
    theirs = shift(ahead, 1)

    attention_cost = cost(
        2 * length * MOST_BLOCKS * BLOCK * width + wide * length * width,
        piece * 3 // 4,
        length * MOST_BLOCKS * BLOCK * width // HD // 2,
    )
    half = length // 2
    early = pl.pallas_call(
        early_attention_kernel,
        out_shape=pltpu.VMEM((rank, half), F32),
        in_specs=[SMEM] + [VMEM] * 3,
        out_specs=VMEM,
        scratch_shapes=[pltpu.VMEM((half, width), BF16)],
        compiler_params=PARAMS,
        cost_estimate=attention_cost,
        name="early_attention",
    )(info, queries, keys_values, down_adapt)
    theirs, early = lax.optimization_barrier((theirs, early))

    grad_part = pl.pallas_call(
        back_gradient_kernel,
        out_shape=vmem((rank, length)),
        in_specs=[VMEM] * 2,
        out_specs=VMEM,
        compiler_params=PARAMS,
        cost_estimate=cost(2 * wide * length * width, piece),
        name="back_gradient",
    )(theirs, grad_inbox)
    grad_part = shift(grad_part, -1)

    def copies(value, count):
        return jnp.broadcast_to(value[None], (count, *value.shape))

    parts = copies(jnp.concatenate([theirs[wide:, length : 2 * length], grad_part], axis=0), tensor_count)
    queries, act_inbox, parts = lax.optimization_barrier((queries, act_inbox, parts))
    arrived = shift(act_inbox, 1)
    parts = lax.all_to_all(parts, "tensor", 0, 0)

    late = pl.pallas_call(
        late_attention_kernel,
        out_shape=pltpu.VMEM((rank, half), F32),
        in_specs=[SMEM] + [VMEM] * 3,
        out_specs=VMEM,
        scratch_shapes=[pltpu.VMEM((half, width), BF16)],
        compiler_params=PARAMS,
        cost_estimate=attention_cost,
        name="late_attention",
    )(info, queries, keys_values, down_adapt)

    fwd_sum = exchange_add(jnp.concatenate([early, late], axis=1), 1)

    pieces = pl.pallas_call(
        contract_kernel,
        out_shape=jax.ShapeDtypeStruct((dp_count, 2 * wide + rank, part), BF16),
        in_specs=[SMEM, VMEM, VMEM, HBM, HBM],
        out_specs=VMEM,
        scratch_shapes=[
            pltpu.VMEM((2, length, width), BF16),
            pltpu.SemaphoreType.DMA((2, 4)),
        ],
        compiler_params=PARAMS,
        cost_estimate=cost(4 * wide * length * width, 2 * piece),
        name="contract",
    )(info, parts, theirs, in_hbm(saved_attn), in_hbm(grad_inbox))
    pieces, fwd_sum = lax.optimization_barrier((pieces, fwd_sum))
    fwd_sum = exchange_add(fwd_sum, 2)
    pieces = lax.all_to_all(pieces, "dp", 0, 0)
    pieces, fwd_sum = lax.optimization_barrier((pieces, fwd_sum))

    down_sum, up_sum = pl.pallas_call(
        collect_kernel,
        out_shape=(vmem((slot_count * rank, part)),) * 2,
        in_specs=[VMEM],
        out_specs=(VMEM, VMEM),
        compiler_params=PARAMS,
        cost_estimate=cost(4 * dp_count * SEGS * slot_count * rank * part, piece // 4),
        name="collect",
    )(pieces)
    up_sum = shift(up_sum, -1)
    sums = copies(jnp.concatenate([down_sum, up_sum], axis=0), dp_count)
    sums, arrived, fwd_sum = lax.optimization_barrier((sums, arrived, fwd_sum))
    fwd_sum = exchange_add(fwd_sum, 4)
    sums = lax.all_to_all(sums, "dp", 0, 0)

    rows = 128
    new_acts = pl.pallas_call(
        hand_on_kernel,
        grid=(length // rows,),
        out_shape=jax.ShapeDtypeStruct(act_inbox.shape, BF16),
        in_specs=[SMEM, pl.BlockSpec((1, rows, width), lambda i: (0, i, 0)), VMEM, VMEM],
        out_specs=pl.BlockSpec((1, rows, width), lambda i: (0, i, 0)),
        compiler_params=PARAMS,
        cost_estimate=cost(2 * wide * length * width, 2 * piece),
        name="hand_on",
    )(info, arrived, fwd_sum, up_adapt)

    sums, new_acts = lax.optimization_barrier((sums, new_acts))
    grad_down, grad_up = pl.pallas_call(
        unpack_kernel,
        out_shape=(jax.ShapeDtypeStruct(up_adapt.shape, BF16),) * 2,
        in_specs=[VMEM],
        out_specs=(VMEM, VMEM),
        compiler_params=PARAMS,
        cost_estimate=cost(0, piece),
        name="unpack",
    )(sums)
    return new_acts, grad_down, grad_up


def solution(mesh):
    placed = (
        P("section", "dp", "tensor"),
        P("section", "dp", "tensor"),
        P("section", "dp", "tensor"),
        P("section", None, "dp", "tensor"),
        P("section", "dp", "tensor"),
        P("section", None, None, "tensor"),
        P("section", None, None, "tensor"),
        P("section", None, "dp", None),
        P("section", None, "dp", None),
        P("section", None, "dp", None),
        P(),
    )
    return jax.shard_map(
        per_device,
        mesh=mesh,
        in_specs=placed,
        out_specs=(
            P("section", "dp", "tensor"),
            P("section", None, None, "tensor"),
            P("section", None, None, "tensor"),
        ),
        check_vma=False,
    )
```

time: 94.1 us -> 80.4 us (0.85)
  blocking collectives: 15.7 us -> 0 us
  local copies, waits for them, and re-layouts: 12.6 us -> 1.8 us
  starting transfers between devices: 20.9 us -> 30.8 us
  Pallas kernels: 13.9 us -> 20.8 us
  waiting for transfers between devices: 29.4 us -> 25.8 us
    all_to_all x1 -> x0, blocking collectives: 15.7 us -> none  [per_device(): pieces = lax.all_to_all(pieces, 'dp', 0, 0)]
    ppermute x0 -> x3, waiting for transfers between devices: none -> 12.4 us  [exchange_add(): lax.ppermute(value, 'tensor', [(i, i ^ distance) for i in range(count)])]
    all_to_all x1, waiting for transfers between devices: 12.2 us -> 2.13 us  [per_device(): parts = lax.all_to_all(parts, 'tensor', 0, 0)]
    unnamed x36 -> x10, local copies, waits for them, and re-layouts: 7.99 us -> 0.02 us
    pallas_call x5 -> x7, Pallas kernels: 9.55 us -> 16.4 us  [the longest x1 4 us: per_device(): pl.pallas_call(contract_kernel, out_shape=jax.ShapeDtypeStruct((dp_count,...]
    all_to_all x1, waiting for transfers between devices: 9.09 us -> 2.27 us  [per_device(): sums = lax.all_to_all(sums, 'dp', 0, 0)]
    all_to_all x0 -> x1, starting transfers between devices: none -> 4.23 us  [per_device(): pieces = lax.all_to_all(pieces, 'dp', 0, 0)]
    ppermute x0 -> x3, starting transfers between devices: none -> 3.62 us  [exchange_add(): lax.ppermute(value, 'tensor', [(i, i ^ distance) for i in range(count)])]
  transfers between devices with their start and end apart: 6 -> 10, of which waited for: 4 -> 8; matrix products, arithmetic and copies ran while one was open for 1% -> 0% of each run, Pallas kernels for 13% -> 20%
where the time goes in v2:
time: 80.4 us; the launch traced here: 80 us
  starting transfers between devices  30.8 us (38%)
  waiting for transfers between devices  25.8 us (32%)
  Pallas kernels  20.8 us (26%)
  local copies, waits for them, and re-layouts  1.8 us (2%)
    ppermute x3, waiting for transfers between devices, exchange_add(): lax.ppermute(value, 'tensor', [(i, i ^ distance) for i in range(count)])  12.4 us
    ppermute x4, starting transfers between devices, shift(): lax.ppermute(value, 'section', [(i, (i + steps) % count) for i in range(c...  11.2 us
    all_to_all x1, starting transfers between devices, per_device(): parts = lax.all_to_all(parts, 'tensor', 0, 0)  8.19 us
    ppermute x4, waiting for transfers between devices, shift(): lax.ppermute(value, 'section', [(i, (i + steps) % count) for i in range(c...  5.88 us
    pallas_call x1, Pallas kernels, per_device(): pl.pallas_call(hand_on_kernel, grid=(length // rows,), out_shape=jax.Shap...  4.39 us
    all_to_all x1, starting transfers between devices, per_device(): pieces = lax.all_to_all(pieces, 'dp', 0, 0)  4.23 us
    pallas_call x1, Pallas kernels, per_device(): pl.pallas_call(contract_kernel, out_shape=jax.ShapeDtypeStruct((dp_count,...  4 us
    ppermute x3, starting transfers between devices, exchange_add(): lax.ppermute(value, 'tensor', [(i, i ^ distance) for i in range(count)])  3.62 us
  transfers between devices with their start and end apart: 10, of which 8 were waited for; matrix products, arithmetic and copies ran while one was open for 0% of the time, Pallas kernels for 20%

profile of v2, /device:TPU:1, one launch (start us, length us, event | category | flops | bytes accessed | tf_op | source)
XLA Modules:
  0.0 80.0 jit_solution(13206701499065735084)
XLA Ops:
  0.7 2.8 %prepare.1 = (bf16[64,2048]{1,0:T(8,128)(2,1)S(1)}, s32[1,18]{1,0:T(1,128)S(1)}) custom-call(s32[1,2,1,3]{3,2,1,0:T(1,128)} %blocks.1, s32[1,2,1,3]{3,2,1,0:T(1,128)} %pads.1, s32[1,2,1,3]{3,2,1,0:T(1,128)} %tenants.1, s32[32]{0:T(128)} %table.1, bf16[1,512,2048]{2,1,0:T(8,128)(2,1)} %saved.3, bf16[1,8,16,2048]{3,2,1,0:T(8,128)(2,1)} %down.5, ...), custom_call_target="tpu_custom_call" | custom-call | flops 100663296 | bytes 10485760 | tf_op jit(solution)/shard_map/prepare/pallas_call | solution.py:291
  3.5 0.0 copy-start.1
  3.5 4.2 %collective-permute-start = (bf16[64,2048]{1,0:T(8,128)(2,1)S(1)}, bf16[64,2048]{1,0:T(8,128)(2,1)S(1)}, u32[]{:S(2)}, u32[]{:S(2)}) collective-permute-start(bf16[64,2048]{1,0:T(8,128)(2,1)S(1)} %get-tuple-element.24), channel_id=1, source_target_pairs={{0,64},{64,128},{128,192},{192,0},{1,65},{65,129},{129,193},{193,1... | collective-permute-start | bytes 786440 | tf_op jit(solution)/shard_map/ppermute | solution.py:260
  7.7 0.0 copy-done
  7.7 3.4 %early_attention.1 = f32[16,256]{1,0:T(8,128)S(1)} custom-call(s32[1,18]{1,0:T(1,128)S(1)} %get-tuple-element.23.info, bf16[1,512,2048]{2,1,0:T(8,128)(2,1)S(1)} %copy-done, bf16[1,2,512,128]{3,2,1,0:T(8,128)(2,1)S(1)} %copy-done.4, bf16[1,8,16,2048]{3,2,1,0:T(8,128)(2,1)S(1)} %copy-done.2), custom_call_target="tpu_custom_call" | custom-call | flops 587202560 | bytes 1572864 | tf_op jit(solution)/shard_map/early_attention/pallas_call | solution.py:316
  11.1 0.0 collective-permute-done.ahead
  11.2 0.7 back_gradient.1
  11.9 3.0 %collective-permute-start.1 = (bf16[16,512]{1,0:T(8,128)(2,1)S(1)}, bf16[16,512]{1,0:T(8,128)(2,1)S(1)}, u32[]{:S(2)}, u32[]{:S(2)}) collective-permute-start(bf16[16,512]{1,0:T(8,128)(2,1)S(1)} %back_gradient.1), channel_id=1, source_target_pairs={{0,192},{64,0},{128,64},{192,128},{1,193},{65,1},{129,65},{193,129... | collective-permute-start | bytes 49160 | tf_op jit(solution)/shard_map/ppermute | solution.py:260
  14.9 2.3 %collective-permute-done.1 = bf16[16,512]{1,0:T(8,128)(2,1)S(1)} collective-permute-done((bf16[16,512]{1,0:T(8,128)(2,1)S(1)}, bf16[16,512]{1,0:T(8,128)(2,1)S(1)}, u32[]{:S(2)}, u32[]{:S(2)}) %collective-permute-start.1) | collective-permute-done | bytes 16416 | tf_op jit(solution)/shard_map/ppermute | solution.py:260
  17.3 0.7 broadcast_in_dim.4
  18.0 0.0 collective-permute-start.5
  18.0 8.2 %all-to-all-start = ((bf16[8,32,512]{2,1,0:T(8,128)(2,1)}), bf16[8,32,512]{2,1,0:T(8,128)(2,1)S(1)}, u32[]{:S(2)}, u32[]{:S(2)}) async-start(bf16[8,32,512]{2,1,0:T(8,128)(2,1)} %broadcast_in_dim.4), calls=%async_computation | async-start | bytes 524288 | tf_op jit(solution)/shard_map/all_to_all | solution.py:345
  26.2 3.4 %late_attention.1 = f32[16,256]{1,0:T(8,128)S(1)} custom-call(s32[1,18]{1,0:T(1,128)S(1)} %get-tuple-element.23.info, bf16[1,512,2048]{2,1,0:T(8,128)(2,1)S(1)} %copy-done, bf16[1,2,512,128]{3,2,1,0:T(8,128)(2,1)S(1)} %copy-done.4, bf16[1,8,16,2048]{3,2,1,0:T(8,128)(2,1)S(1)} %copy-done.2), custom_call_target="tpu_custom_call" | custom-call | flops 587202560 | bytes 1572864 | tf_op jit(solution)/shard_map/late_attention/pallas_call | solution.py:347
  29.6 1.5 %collective-permute-start.2 = (f32[16,512]{1,0:T(8,128)S(1)}, f32[16,512]{1,0:T(8,128)S(1)}, u32[]{:S(2)}, u32[]{:S(2)}) collective-permute-start(f32[16,512]{1,0:T(8,128)S(1)} %pad_maximum_fusion.2), channel_id=1, source_target_pairs={{0,8},{8,0},{16,24},{24,16},{32,40},{40,32},{48,56},{56,48},{1,9},... | collective-permute-start | bytes 98312 | tf_op jit(solution)/shard_map/ppermute | solution.py:265
  31.2 3.6 %collective-permute-done.2 = f32[16,512]{1,0:T(8,128)S(1)} collective-permute-done((f32[16,512]{1,0:T(8,128)S(1)}, f32[16,512]{1,0:T(8,128)S(1)}, u32[]{:S(2)}, u32[]{:S(2)}) %collective-permute-start.2) | collective-permute-done | bytes 32800 | tf_op jit(solution)/shard_map/ppermute | solution.py:265
  34.8 2.1 %all-to-all-done.parts = bf16[8,32,512]{2,1,0:T(8,128)(2,1)S(1)} async-done(((bf16[8,32,512]{2,1,0:T(8,128)(2,1)}), bf16[8,32,512]{2,1,0:T(8,128)(2,1)S(1)}, u32[]{:S(2)}, u32[]{:S(2)}) %all-to-all-start) | async-done | bytes 262176 | tf_op jit(solution)/shard_map/all_to_all | solution.py:345
  36.9 4.0 %contract.1 = bf16[8,112,256]{2,1,0:T(8,128)(2,1)} custom-call(s32[1,18]{1,0:T(1,128)S(1)} %get-tuple-element.23.info, bf16[8,32,512]{2,1,0:T(8,128)(2,1)S(1)} %all-to-all-done.parts, bf16[64,2048]{1,0:T(8,128)(2,1)S(1)} %collective-permute-done.ahead, bf16[1,512,2048]{2,1,0:T(8,128)(2,1)} %saved.3, bf16[1,512,2048]{2,1,0:T(8,128)(2,1)} %grads.3), custom_call_target="tpu_custom_call" | custom-call | flops 201326592 | bytes 4194304 | tf_op jit(solution)/shard_map/contract/pallas_call | solution.py:360
  40.9 4.2 %all-to-all-start.1 = ((bf16[8,112,256]{2,1,0:T(8,128)(2,1)}), bf16[8,112,256]{2,1,0:T(8,128)(2,1)S(1)}, u32[]{:S(2)}, u32[]{:S(2)}) async-start(bf16[8,112,256]{2,1,0:T(8,128)(2,1)} %contract.1), calls=%async_computation.1 | async-start | bytes 917504 | tf_op jit(solution)/shard_map/all_to_all | solution.py:375
  45.2 0.1 collective-permute-start.3
  45.3 3.7 %collective-permute-done.3 = f32[16,512]{1,0:T(8,128)S(1)} collective-permute-done((f32[16,512]{1,0:T(8,128)S(1)}, f32[16,512]{1,0:T(8,128)S(1)}, u32[]{:S(2)}, u32[]{:S(2)}) %collective-permute-start.3) | collective-permute-done | bytes 32800 | tf_op jit(solution)/shard_map/ppermute | solution.py:265
  48.9 3.1 %all-to-all-done.1.pieces = bf16[8,112,256]{2,1,0:T(8,128)(2,1)S(1)} async-done(((bf16[8,112,256]{2,1,0:T(8,128)(2,1)}), bf16[8,112,256]{2,1,0:T(8,128)(2,1)S(1)}, u32[]{:S(2)}, u32[]{:S(2)}) %all-to-all-start.1) | async-done | bytes 458784 | tf_op jit(solution)/shard_map/all_to_all | solution.py:375
  52.0 1.0 %collect.1 = (bf16[128,256]{1,0:T(8,128)(2,1)S(1)}, bf16[128,256]{1,0:T(8,128)(2,1)S(1)}) custom-call(bf16[8,112,256]{2,1,0:T(8,128)(2,1)S(1)} %all-to-all-done.1.pieces), custom_call_target="tpu_custom_call" | custom-call | flops 3145728 | bytes 524288 | tf_op jit(solution)/shard_map/collect/pallas_call | solution.py:378
  53.0 4.0 %collective-permute-start.4 = (bf16[128,256]{1,0:T(8,128)(2,1)S(1)}, bf16[128,256]{1,0:T(8,128)(2,1)S(1)}, u32[]{:S(2)}, u32[]{:S(2)}) collective-permute-start(bf16[128,256]{1,0:T(8,128)(2,1)S(1)} %get-tuple-element.33), channel_id=1, source_target_pairs={{0,192},{64,0},{128,64},{192,128},{1,193},{65,1},{129,65},{193,129... | collective-permute-start | bytes 196616 | tf_op jit(solution)/shard_map/ppermute | solution.py:260
  57.0 3.6 %collective-permute-done.4 = bf16[128,256]{1,0:T(8,128)(2,1)S(1)} collective-permute-done((bf16[128,256]{1,0:T(8,128)(2,1)S(1)}, bf16[128,256]{1,0:T(8,128)(2,1)S(1)}, u32[]{:S(2)}, u32[]{:S(2)}) %collective-permute-start.4) | collective-permute-done | bytes 65568 | tf_op jit(solution)/shard_map/ppermute | solution.py:260
  60.5 0.0 collective-permute-done.5.arrived
  60.5 1.0 %broadcast_in_dim.5 = bf16[8,256,256]{2,1,0:T(8,128)(2,1)} broadcast(bf16[256,256]{1,0:T(8,128)(2,1)S(1)} %pad_maximum_fusion), dimensions={1,2} | broadcast | bytes 1179648 | tf_op jit(solution)/shard_map/broadcast_in_dim | solution.py:340
  61.6 3.6 %all-to-all-start.2 = ((bf16[8,256,256]{2,1,0:T(8,128)(2,1)}), bf16[8,256,256]{2,1,0:T(8,128)(2,1)S(1)}, u32[]{:S(2)}, u32[]{:S(2)}) async-start(bf16[8,256,256]{2,1,0:T(8,128)(2,1)} %broadcast_in_dim.5), calls=%async_computation.2 | async-start | bytes 2097152 | tf_op jit(solution)/shard_map/all_to_all | solution.py:391
  65.2 2.0 %collective-permute-start.6 = (f32[16,512]{1,0:T(8,128)S(1)}, f32[16,512]{1,0:T(8,128)S(1)}, u32[]{:S(2)}, u32[]{:S(2)}) collective-permute-start(f32[16,512]{1,0:T(8,128)S(1)} %add.10), channel_id=1, source_target_pairs={{0,32},{8,40},{16,48},{24,56},{32,0},{40,8},{48,16},{56,24},{1,33}... | collective-permute-start | bytes 98312 | tf_op jit(solution)/shard_map/ppermute | solution.py:265
  67.1 5.1 %collective-permute-done.6 = f32[16,512]{1,0:T(8,128)S(1)} collective-permute-done((f32[16,512]{1,0:T(8,128)S(1)}, f32[16,512]{1,0:T(8,128)S(1)}, u32[]{:S(2)}, u32[]{:S(2)}) %collective-permute-start.6) | collective-permute-done | bytes 32800 | tf_op jit(solution)/shard_map/ppermute | solution.py:265
  72.3 4.4 %hand_on.1 = bf16[1,512,2048]{2,1,0:T(8,128)(2,1)} custom-call(s32[1,18]{1,0:T(1,128)S(1)} %get-tuple-element.23.info, bf16[1,512,2048]{2,1,0:T(8,128)(2,1)} %collective-permute-done.5.arrived, f32[16,512]{1,0:T(8,128)S(1)} %add.11.fwd, bf16[1,8,16,2048]{3,2,1,0:T(8,128)(2,1)S(1)} %copy-done.3), custom_call_target="tpu_custom_call" | custom-call | flops 100663296 | bytes 4194304 | tf_op jit(solution)/shard_map/hand_on/pallas_call | solution.py:394
  76.7 2.3 %all-to-all-done.2.sums = bf16[8,256,256]{2,1,0:T(8,128)(2,1)S(1)} async-done(((bf16[8,256,256]{2,1,0:T(8,128)(2,1)}), bf16[8,256,256]{2,1,0:T(8,128)(2,1)S(1)}, u32[]{:S(2)}, u32[]{:S(2)}) %all-to-all-start.2) | async-done | bytes 1048608 | tf_op jit(solution)/shard_map/all_to_all | solution.py:391
  78.9 1.1 %unpack.1 = (bf16[1,8,16,2048]{3,2,1,0:T(8,128)(2,1)}, bf16[1,8,16,2048]{3,2,1,0:T(8,128)(2,1)}) custom-call(bf16[8,256,256]{2,1,0:T(8,128)(2,1)S(1)} %all-to-all-done.2.sums), custom_call_target="tpu_custom_call" | custom-call | bytes 2097152 | tf_op jit(solution)/shard_map/unpack/pallas_call | solution.py:406
  (15 shorter events, 0.1 us)
Async XLA Ops:
  0.6 7.1 %copy-start.2 = (bf16[1,8,16,2048]{3,2,1,0:T(8,128)(2,1)S(1)}, bf16[1,8,16,2048]{3,2,1,0:T(8,128)(2,1)}, u32[]{:S(2)}) copy-start(bf16[1,8,16,2048]{3,2,1,0:T(8,128)(2,1)} %down.5) | copy-start | bytes 1572868
  0.6 7.1 %copy-start.4 = (bf16[1,2,512,128]{3,2,1,0:T(8,128)(2,1)S(1)}, bf16[1,2,512,128]{3,2,1,0:T(8,128)(2,1)}, u32[]{:S(2)}) copy-start(bf16[1,2,512,128]{3,2,1,0:T(8,128)(2,1)} %keys_values.3) | copy-start | bytes 786436
  0.7 7.1 %copy-start = (bf16[1,512,2048]{2,1,0:T(8,128)(2,1)S(1)}, bf16[1,512,2048]{2,1,0:T(8,128)(2,1)}, u32[]{:S(2)}) copy-start(bf16[1,512,2048]{2,1,0:T(8,128)(2,1)} %queries.2) | copy-start | bytes 6291460
  3.5 7.7 %copy-start.1 = (bf16[1,512,2048]{2,1,0:T(8,128)(2,1)S(1)}, bf16[1,512,2048]{2,1,0:T(8,128)(2,1)}, u32[]{:S(2)}) copy-start(bf16[1,512,2048]{2,1,0:T(8,128)(2,1)} %grads.3) | copy-start | bytes 6291460
  3.5 7.6 %collective-permute-start = (bf16[64,2048]{1,0:T(8,128)(2,1)S(1)}, bf16[64,2048]{1,0:T(8,128)(2,1)S(1)}, u32[]{:S(2)}, u32[]{:S(2)}) collective-permute-start(bf16[64,2048]{1,0:T(8,128)(2,1)S(1)} %get-tuple-element.24), channel_id=1, source_target_pairs={{0,64},{64,128},{128,192},{192,0},{1,65},{65,129},{129,193},{193,1... | collective-permute-start | bytes 786440 | tf_op jit(solution)/shard_map/ppermute | solution.py:260
  11.9 5.4 %collective-permute-start.1 = (bf16[16,512]{1,0:T(8,128)(2,1)S(1)}, bf16[16,512]{1,0:T(8,128)(2,1)S(1)}, u32[]{:S(2)}, u32[]{:S(2)}) collective-permute-start(bf16[16,512]{1,0:T(8,128)(2,1)S(1)} %back_gradient.1), channel_id=1, source_target_pairs={{0,192},{64,0},{128,64},{192,128},{1,193},{65,1},{129,65},{193,129... | collective-permute-start | bytes 49160 | tf_op jit(solution)/shard_map/ppermute | solution.py:260
  18.0 42.5 %collective-permute-start.5 = (bf16[1,512,2048]{2,1,0:T(8,128)(2,1)}, bf16[1,512,2048]{2,1,0:T(8,128)(2,1)}, u32[]{:S(2)}, u32[]{:S(2)}) collective-permute-start(bf16[1,512,2048]{2,1,0:T(8,128)(2,1)} %param.11), channel_id=1, source_target_pairs={{0,64},{64,128},{128,192},{192,0},{1,65},{65,129},{129,193},{193,1... | collective-permute-start | bytes 6291464 | tf_op jit(solution)/shard_map/ppermute | solution.py:260
  18.0 18.9 %all-to-all-start = ((bf16[8,32,512]{2,1,0:T(8,128)(2,1)}), bf16[8,32,512]{2,1,0:T(8,128)(2,1)S(1)}, u32[]{:S(2)}, u32[]{:S(2)}) async-start(bf16[8,32,512]{2,1,0:T(8,128)(2,1)} %broadcast_in_dim.4), calls=%async_computation | async-start | bytes 524288 | tf_op jit(solution)/shard_map/all_to_all | solution.py:345
  29.6 5.2 %collective-permute-start.2 = (f32[16,512]{1,0:T(8,128)S(1)}, f32[16,512]{1,0:T(8,128)S(1)}, u32[]{:S(2)}, u32[]{:S(2)}) collective-permute-start(f32[16,512]{1,0:T(8,128)S(1)} %pad_maximum_fusion.2), channel_id=1, source_target_pairs={{0,8},{8,0},{16,24},{24,16},{32,40},{40,32},{48,56},{56,48},{1,9},... | collective-permute-start | bytes 98312 | tf_op jit(solution)/shard_map/ppermute | solution.py:265
  40.9 11.1 %all-to-all-start.1 = ((bf16[8,112,256]{2,1,0:T(8,128)(2,1)}), bf16[8,112,256]{2,1,0:T(8,128)(2,1)S(1)}, u32[]{:S(2)}, u32[]{:S(2)}) async-start(bf16[8,112,256]{2,1,0:T(8,128)(2,1)} %contract.1), calls=%async_computation.1 | async-start | bytes 917504 | tf_op jit(solution)/shard_map/all_to_all | solution.py:375
  45.2 27.1 %copy-start.3 = (bf16[1,8,16,2048]{3,2,1,0:T(8,128)(2,1)S(1)}, bf16[1,8,16,2048]{3,2,1,0:T(8,128)(2,1)}, u32[]{:S(2)}) copy-start(bf16[1,8,16,2048]{3,2,1,0:T(8,128)(2,1)} %up.3) | copy-start | bytes 1572868
  45.2 3.8 %collective-permute-start.3 = (f32[16,512]{1,0:T(8,128)S(1)}, f32[16,512]{1,0:T(8,128)S(1)}, u32[]{:S(2)}, u32[]{:S(2)}) collective-permute-start(f32[16,512]{1,0:T(8,128)S(1)} %fusion), channel_id=1, source_target_pairs={{0,16},{8,24},{16,0},{24,8},{32,48},{40,56},{48,32},{56,40},{1,17}... | collective-permute-start | bytes 98312 | tf_op jit(solution)/shard_map/ppermute | solution.py:265
  53.0 7.5 %collective-permute-start.4 = (bf16[128,256]{1,0:T(8,128)(2,1)S(1)}, bf16[128,256]{1,0:T(8,128)(2,1)S(1)}, u32[]{:S(2)}, u32[]{:S(2)}) collective-permute-start(bf16[128,256]{1,0:T(8,128)(2,1)S(1)} %get-tuple-element.33), channel_id=1, source_target_pairs={{0,192},{64,0},{128,64},{192,128},{1,193},{65,1},{129,65},{193,129... | collective-permute-start | bytes 196616 | tf_op jit(solution)/shard_map/ppermute | solution.py:260
  61.6 17.3 %all-to-all-start.2 = ((bf16[8,256,256]{2,1,0:T(8,128)(2,1)}), bf16[8,256,256]{2,1,0:T(8,128)(2,1)S(1)}, u32[]{:S(2)}, u32[]{:S(2)}) async-start(bf16[8,256,256]{2,1,0:T(8,128)(2,1)} %broadcast_in_dim.5), calls=%async_computation.2 | async-start | bytes 2097152 | tf_op jit(solution)/shard_map/all_to_all | solution.py:391
  65.2 7.1 %collective-permute-start.6 = (f32[16,512]{1,0:T(8,128)S(1)}, f32[16,512]{1,0:T(8,128)S(1)}, u32[]{:S(2)}, u32[]{:S(2)}) collective-permute-start(f32[16,512]{1,0:T(8,128)S(1)} %add.10), channel_id=1, source_target_pairs={{0,32},{8,40},{16,48},{24,56},{32,0},{40,8},{48,16},{56,24},{1,33}... | collective-permute-start | bytes 98312 | tf_op jit(solution)/shard_map/ppermute | solution.py:265

commit v3 on v2

--- a/solution.py
+++ b/solution.py
@@ -14,6 +14,7 @@
 ADAPTER_SCALE = 2.0
 BF16 = jnp.bfloat16
 F32 = jnp.float32
+TENSOR = ("z4", "zi")
 SMEM = pl.BlockSpec(memory_space=pltpu.SMEM)
 VMEM = pl.BlockSpec(memory_space=pltpu.VMEM)
 HBM = pl.BlockSpec(memory_space=pltpu.HBM)
@@ -62,19 +63,14 @@
     _, _, rank, width = up.shape
     length = saved.shape[1]
     wide = SEGS * rank
-    cuts = sems.shape[0] - 6
-    tall = length // cuts
     first = [pltpu.make_async_copy(src, raw.at[i], sems.at[i]) for i, src in enumerate((blocks, pads, tenants))]
     first.append(pltpu.make_async_copy(table, listed, sems.at[3]))
     adapters = [
         pltpu.make_async_copy(up, ups, sems.at[4]),
         pltpu.make_async_copy(down, downs, sems.at[5]),
     ]
-    later = []
-    for i in range(cuts):
-        at = pl.ds(tall * i, tall)
-        later.append(pltpu.make_async_copy(saved.at[0, at], held.at[at], sems.at[6 + i]))
-    for copy in first + later + adapters:
+    tokens = pltpu.make_async_copy(saved.at[0], held, sems.at[6])
+    for copy in first + [tokens] + adapters:
         copy.start()
     for copy in first:
         copy.wait()
@@ -91,17 +87,16 @@
         notes = jnp.where((row == i) & masks[i], 1.0, notes)
         notes = jnp.where(row == SEGS + i, slots[i].astype(F32), notes)
     out[wide:, :length] = notes.astype(BF16)
-    out[wide:, 2 * length :] = jnp.zeros((rank, width - 2 * length), BF16)
+    out[wide:, 3 * length :] = jnp.zeros((rank, width - 3 * length), BF16)
     adapters[0].wait()
     for i in range(SEGS):
         out[rank * i : rank * (i + 1), :] = ups[0, slots[i]]
     adapters[1].wait()
-    rows = pick_rows(downs, slots)
-    for i, copy in enumerate(later):
-        copy.wait()
-        at = slice(tall * i, tall * (i + 1))
-        back = fold(rows_by_rows(rows, held[at]), [m[:, at] for m in masks], rank)
-        out[wide:, length + tall * i : length + tall * (i + 1)] = back.astype(BF16)
+    tokens.wait()
+    ranks = fold(rows_by_rows(pick_rows(downs, slots), held[...]), masks, rank)
+    high = ranks.astype(BF16)
+    out[wide:, length : 2 * length] = high
+    out[wide:, 2 * length : 3 * length] = (ranks - high.astype(F32)).astype(BF16)
 
 
 def recall(info, batch):
@@ -118,7 +113,7 @@
     rank, length = out.shape
     wide = SEGS * rank
     full = rows_by_rows(ahead[:wide, :], grads[0])
-    out[...] = fold(full, note_masks(ahead, wide, length), rank).astype(BF16)
+    out[...] = fold(full, note_masks(ahead, wide, length), rank)
 
 
 def attend_blocks(info, queries, keys_values, attended, first, last, base):
@@ -226,9 +221,29 @@
     return (scale * total).reshape(rows, width).astype(BF16)
 
 
-def collect_kernel(pieces, down_out, up_out):
-    down_out[...] = collect(pieces, 0, 1.0, down_out.shape[0])
-    up_out[...] = collect(pieces, 1, ADAPTER_SCALE, up_out.shape[0])
+def collect_up_kernel(pieces, out):
+    out[...] = collect(pieces, 1, ADAPTER_SCALE, out.shape[0])
+
+
+def copy_to_all(block, out, first, sems):
+    rows = block.shape[0]
+    copies = [
+        pltpu.make_async_copy(block, out.at[d, pl.ds(first, rows)], sems.at[d]) for d in range(out.shape[0])
+    ]
+    for copy in copies:
+        copy.start()
+    for copy in copies:
+        copy.wait()
+
+
+def collect_down_kernel(pieces, out, block, sems):
+    block[...] = collect(pieces, 0, 1.0, block.shape[0])
+    copy_to_all(block, out, 0, sems)
+
+
+def add_up_kernel(block, half, out, sems):
+    del half
+    copy_to_all(block, out, block.shape[0], sems)
 
 
 def unpack_kernel(sums, down_out, up_out):
@@ -261,8 +276,8 @@
 
 
 def exchange_add(value, distance):
-    count = lax.axis_size("tensor")
-    return value + lax.ppermute(value, "tensor", [(i, i ^ distance) for i in range(count)])
+    count = lax.axis_size(TENSOR)
+    return value + lax.ppermute(value, TENSOR, [(i, i ^ distance) for i in range(count)])
 
 
 def per_device(
@@ -282,11 +297,10 @@
     _, slot_count, rank, _ = up_adapt.shape
     wide = SEGS * rank
     scalars = (seg_blocks, seg_pads, seg_tenant, adapter_table)
-    tensor_count, dp_count = lax.axis_size("tensor"), lax.axis_size("dp")
+    dp_count = lax.axis_size("dp")
     part = width // dp_count
     piece = length * width * 2
 
-    cuts = 1
     vmem = lambda shape: pltpu.VMEM(shape, BF16)
     ahead, info = pl.pallas_call(
         prepare_kernel,
@@ -299,7 +313,7 @@
             pltpu.VMEM((length, width), BF16),
             pltpu.VMEM(down_adapt.shape, BF16),
             pltpu.VMEM(up_adapt.shape, BF16),
-            pltpu.SemaphoreType.DMA((6 + cuts,)),
+            pltpu.SemaphoreType.DMA((7,)),
         ],
         compiler_params=PARAMS,
         cost_estimate=cost(2 * wide * length * width, 5 * piece),
@@ -327,7 +341,7 @@
 
     grad_part = pl.pallas_call(
         back_gradient_kernel,
-        out_shape=vmem((rank, length)),
+        out_shape=pltpu.VMEM((rank, length), F32),
         in_specs=[VMEM] * 2,
         out_specs=VMEM,
         compiler_params=PARAMS,
@@ -339,11 +353,11 @@
     def copies(value, count):
         return jnp.broadcast_to(value[None], (count, *value.shape))
 
-    parts = copies(jnp.concatenate([theirs[wide:, length : 2 * length], grad_part], axis=0), tensor_count)
+    back = theirs[wide:, length : 2 * length].astype(F32) + theirs[wide:, 2 * length : 3 * length].astype(F32)
+    parts = jnp.concatenate([back, grad_part], axis=0)
     queries, act_inbox, parts = lax.optimization_barrier((queries, act_inbox, parts))
+    parts = exchange_add(parts, 4).astype(BF16)
     arrived = shift(act_inbox, 1)
-    parts = lax.all_to_all(parts, "tensor", 0, 0)
-
     late = pl.pallas_call(
         late_attention_kernel,
         out_shape=pltpu.VMEM((rank, half), F32),
@@ -354,6 +368,8 @@
         cost_estimate=attention_cost,
         name="late_attention",
     )(info, queries, keys_values, down_adapt)
+    parts, late = lax.optimization_barrier((parts, late))
+    parts = lax.all_to_all(copies(parts, lax.axis_size("zi")), "zi", 0, 0)
 
     fwd_sum = exchange_add(jnp.concatenate([early, late], axis=1), 1)
 
@@ -375,17 +391,39 @@
     pieces = lax.all_to_all(pieces, "dp", 0, 0)
     pieces, fwd_sum = lax.optimization_barrier((pieces, fwd_sum))
 
-    down_sum, up_sum = pl.pallas_call(
-        collect_kernel,
-        out_shape=(vmem((slot_count * rank, part)),) * 2,
+    rows = slot_count * rank
+    up_sum = pl.pallas_call(
+        collect_up_kernel,
+        out_shape=vmem((rows, part)),
         in_specs=[VMEM],
-        out_specs=(VMEM, VMEM),
-        compiler_params=PARAMS,
-        cost_estimate=cost(4 * dp_count * SEGS * slot_count * rank * part, piece // 4),
-        name="collect",
+        out_specs=VMEM,
+        compiler_params=PARAMS,
+        cost_estimate=cost(2 * dp_count * SEGS * rows * part, piece // 4),
+        name="collect_up",
     )(pieces)
-    up_sum = shift(up_sum, -1)
-    sums = copies(jnp.concatenate([down_sum, up_sum], axis=0), dp_count)
+    pieces, up_sum = lax.optimization_barrier((pieces, up_sum))
+    sums_shape = jax.ShapeDtypeStruct((dp_count, 2 * rows, part), BF16)
+    sums = pl.pallas_call(
+        collect_down_kernel,
+        out_shape=sums_shape,
+        in_specs=[VMEM],
+        out_specs=HBM,
+        scratch_shapes=[pltpu.VMEM((rows, part), BF16), pltpu.SemaphoreType.DMA((dp_count,))],
+        compiler_params=PARAMS,
+        cost_estimate=cost(2 * dp_count * SEGS * rows * part, piece // 2),
+        name="collect_down",
+    )(pieces)
+    sums = pl.pallas_call(
+        add_up_kernel,
+        out_shape=sums_shape,
+        in_specs=[VMEM, HBM],
+        out_specs=HBM,
+        scratch_shapes=[pltpu.SemaphoreType.DMA((dp_count,))],
+        input_output_aliases={1: 0},
+        compiler_params=PARAMS,
+        cost_estimate=cost(0, piece // 4),
+        name="add_up",
+    )(shift(up_sum, -1), sums)
     sums, arrived, fwd_sum = lax.optimization_barrier((sums, arrived, fwd_sum))
     fwd_sum = exchange_add(fwd_sum, 4)
     sums = lax.all_to_all(sums, "dp", 0, 0)
@@ -416,27 +454,27 @@
 
 
 def solution(mesh):
-    placed = (
-        P("section", "dp", "tensor"),
-        P("section", "dp", "tensor"),
-        P("section", "dp", "tensor"),
-        P("section", None, "dp", "tensor"),
-        P("section", "dp", "tensor"),
-        P("section", None, None, "tensor"),
-        P("section", None, None, "tensor"),
-        P("section", None, "dp", None),
-        P("section", None, "dp", None),
-        P("section", None, "dp", None),
-        P(),
-    )
+    section, tensor, dp = (mesh.shape[name] for name in ("section", "tensor", "dp"))
+    fine = jax.sharding.Mesh(mesh.devices.reshape(section, 2, tensor // 2, dp), ("section", *TENSOR, "dp"))
+    rows = P("section", "dp", TENSOR)
+    adapters = P("section", None, None, TENSOR)
+    scalars = P("section", None, "dp", None)
     return jax.shard_map(
         per_device,
-        mesh=mesh,
-        in_specs=placed,
-        out_specs=(
-            P("section", "dp", "tensor"),
-            P("section", None, None, "tensor"),
-            P("section", None, None, "tensor"),
+        mesh=fine,
+        in_specs=(
+            rows,
+            rows,
+            rows,
+            P("section", None, "dp", TENSOR),
+            rows,
+            adapters,
+            adapters,
+            scalars,
+            scalars,
+            scalars,
+            P(),
         ),
+        out_specs=(rows, adapters, adapters),
         check_vma=False,
     )

time: 80.4 us -> 79.1 us (0.984)
  waiting for transfers between devices: 25.8 us -> 18.3 us
  starting transfers between devices: 30.8 us -> 36.5 us
    ppermute x3 -> x4, starting transfers between devices: 3.62 us -> 14.8 us  [exchange_add(): lax.ppermute(value, TENSOR, [(i, i ^ distance) for i in range(count)])]
    ppermute x3 -> x4, waiting for transfers between devices: 12.4 us -> 6.18 us  [exchange_add(): lax.ppermute(value, TENSOR, [(i, i ^ distance) for i in range(count)])]
    all_to_all x1, starting transfers between devices: 8.19 us -> 3.33 us  [per_device(): parts = lax.all_to_all(copies(parts, lax.axis_size('zi')), 'zi', 0, 0)]
    pallas_call x2 -> x4, Pallas kernels: 1.7 us -> 3.47 us  [the longest x1 1.36 us: per_device(): pl.pallas_call(collect_down_kernel, out_shape=sums_shape, in_specs=[VMEM]...]
    pallas_call x1, Pallas kernels: 4.39 us -> 3.13 us  [per_device(): pl.pallas_call(hand_on_kernel, grid=(length // rows,), out_shape=jax.Shap...]
    ppermute x4, waiting for transfers between devices: 5.88 us -> 4.69 us  [shift(): lax.ppermute(value, 'section', [(i, (i + steps) % count) for i in range(c...]
    broadcast_in_dim x2 -> x1, local copies, waits for them, and re-layouts: 1.78 us -> 0.66 us  [copies(): return jnp.broadcast_to(value[None], (count, *value.shape))]
    unnamed x10 -> x11, local copies, waits for them, and re-layouts: 0.02 us -> 1.06 us
  transfers between devices with their start and end apart: 10 -> 11, of which waited for: 8 -> 8; matrix products, arithmetic and copies ran while one was open for 0% -> 1% of each run, Pallas kernels for 20% -> 21%
where the time goes in v3:
time: 79.1 us; the launch traced here: 78.8 us
  starting transfers between devices  36.5 us (46%)
  Pallas kernels  21.3 us (27%)
  waiting for transfers between devices  18.3 us (23%)
  local copies, waits for them, and re-layouts  1.73 us (2%)
  between operations  0.82 us (1%)
    ppermute x4, starting transfers between devices, exchange_add(): lax.ppermute(value, TENSOR, [(i, i ^ distance) for i in range(count)])  14.8 us
    ppermute x4, starting transfers between devices, shift(): lax.ppermute(value, 'section', [(i, (i + steps) % count) for i in range(c...  10.6 us
    ppermute x4, waiting for transfers between devices, exchange_add(): lax.ppermute(value, TENSOR, [(i, i ^ distance) for i in range(count)])  6.18 us
    ppermute x4, waiting for transfers between devices, shift(): lax.ppermute(value, 'section', [(i, (i + steps) % count) for i in range(c...  4.69 us
    all_to_all x1, starting transfers between devices, per_device(): pieces = lax.all_to_all(pieces, 'dp', 0, 0)  4.19 us
    pallas_call x1, Pallas kernels, per_device(): pl.pallas_call(contract_kernel, out_shape=jax.ShapeDtypeStruct((dp_count,...  4 us
    all_to_all x1, starting transfers between devices, per_device(): sums = lax.all_to_all(sums, 'dp', 0, 0)  3.57 us
    pallas_call x1, Pallas kernels, per_device(): pl.pallas_call(late_attention_kernel, out_shape=pltpu.VMEM((rank, half),...  3.42 us
  transfers between devices with their start and end apart: 11, of which 8 were waited for; matrix products, arithmetic and copies ran while one was open for 1% of the time, Pallas kernels for 21%

profile of v3, /device:TPU:1, one launch (start us, length us, event | category | flops | bytes accessed | tf_op | source)
XLA Modules:
  0.0 78.8 jit_solution(7583604317369668014)
XLA Ops:
  0.7 2.8 %prepare.1 = (bf16[64,2048]{1,0:T(8,128)(2,1)S(1)}, s32[1,18]{1,0:T(1,128)S(1)}) custom-call(s32[1,2,1,3]{3,2,1,0:T(1,128)} %blocks.1, s32[1,2,1,3]{3,2,1,0:T(1,128)} %pads.1, s32[1,2,1,3]{3,2,1,0:T(1,128)} %tenants.1, s32[32]{0:T(128)} %table.1, bf16[1,512,2048]{2,1,0:T(8,128)(2,1)} %saved.3, bf16[1,8,16,2048]{3,2,1,0:T(8,128)(2,1)} %down.5, ...), custom_call_target="tpu_custom_call" | custom-call | flops 100663296 | bytes 10485760 | tf_op jit(solution)/shard_map/prepare/pallas_call | solution.py:305
  3.5 0.0 copy-start.1
  3.5 4.2 %collective-permute-start = (bf16[64,2048]{1,0:T(8,128)(2,1)S(1)}, bf16[64,2048]{1,0:T(8,128)(2,1)S(1)}, u32[]{:S(2)}, u32[]{:S(2)}) collective-permute-start(bf16[64,2048]{1,0:T(8,128)(2,1)S(1)} %get-tuple-element.26), channel_id=1, source_target_pairs={{0,64},{64,128},{128,192},{192,0},{1,65},{65,129},{129,193},{193,1... | collective-permute-start | bytes 786440 | tf_op jit(solution)/shard_map/ppermute | solution.py:275
  7.7 3.4 %early_attention.1 = f32[16,256]{1,0:T(8,128)S(1)} custom-call(s32[1,18]{1,0:T(1,128)S(1)} %get-tuple-element.25.info, bf16[1,512,2048]{2,1,0:T(8,128)(2,1)S(1)} %copy-done, bf16[1,2,512,128]{3,2,1,0:T(8,128)(2,1)S(1)} %copy-done.4, bf16[1,8,16,2048]{3,2,1,0:T(8,128)(2,1)S(1)} %copy-done.2), custom_call_target="tpu_custom_call" | custom-call | flops 587202560 | bytes 1572864 | tf_op jit(solution)/shard_map/early_attention/pallas_call | solution.py:330
  11.2 0.7 back_gradient.1
  11.9 3.0 %collective-permute-start.1 = (f32[16,512]{1,0:T(8,128)S(1)}, f32[16,512]{1,0:T(8,128)S(1)}, u32[]{:S(2)}, u32[]{:S(2)}) collective-permute-start(f32[16,512]{1,0:T(8,128)S(1)} %back_gradient.1), channel_id=1, source_target_pairs={{0,192},{64,0},{128,64},{192,128},{1,193},{65,1},{129,65},{193,129... | collective-permute-start | bytes 98312 | tf_op jit(solution)/shard_map/ppermute | solution.py:275
  14.9 2.5 %collective-permute-done.1 = f32[16,512]{1,0:T(8,128)S(1)} collective-permute-done((f32[16,512]{1,0:T(8,128)S(1)}, f32[16,512]{1,0:T(8,128)S(1)}, u32[]{:S(2)}, u32[]{:S(2)}) %collective-permute-start.1) | collective-permute-done | bytes 32800 | tf_op jit(solution)/shard_map/ppermute | solution.py:275
  17.4 0.0 collective-permute-start.6
  17.4 7.0 %collective-permute-start.2 = (f32[32,512]{1,0:T(8,128)S(1)}, f32[32,512]{1,0:T(8,128)S(1)}, u32[]{:S(2)}, u32[]{:S(2)}) collective-permute-start(f32[32,512]{1,0:T(8,128)S(1)} %pad_maximum_fusion), channel_id=1, source_target_pairs={{0,32},{8,40},{16,48},{24,56},{32,0},{40,8},{48,16},{56,24},{1,33}... | collective-permute-start | bytes 196616 | tf_op jit(solution)/shard_map/ppermute | solution.py:280
  24.4 3.4 %late_attention.1 = f32[16,256]{1,0:T(8,128)S(1)} custom-call(s32[1,18]{1,0:T(1,128)S(1)} %get-tuple-element.25.info, bf16[1,512,2048]{2,1,0:T(8,128)(2,1)S(1)} %copy-done, bf16[1,2,512,128]{3,2,1,0:T(8,128)(2,1)S(1)} %copy-done.4, bf16[1,8,16,2048]{3,2,1,0:T(8,128)(2,1)S(1)} %copy-done.2), custom_call_target="tpu_custom_call" | custom-call | flops 587202560 | bytes 1572864 | tf_op jit(solution)/shard_map/late_attention/pallas_call | solution.py:361
  27.9 0.7 broadcast_in_dim.2
  28.6 3.3 %all-to-all-start = ((bf16[4,32,512]{2,1,0:T(8,128)(2,1)}), bf16[4,32,512]{2,1,0:T(8,128)(2,1)S(1)}, u32[]{:S(2)}, u32[]{:S(2)}) async-start(bf16[4,32,512]{2,1,0:T(8,128)(2,1)} %broadcast_in_dim.2), calls=%async_computation | async-start | bytes 262144 | tf_op jit(solution)/shard_map/all_to_all | solution.py:372
  31.9 1.4 %collective-permute-start.3 = (f32[16,512]{1,0:T(8,128)S(1)}, f32[16,512]{1,0:T(8,128)S(1)}, u32[]{:S(2)}, u32[]{:S(2)}) collective-permute-start(f32[16,512]{1,0:T(8,128)S(1)} %constant_dynamic-update-slice_fusion), channel_id=1, source_target_pairs={{0,8},{8,0},{16,24},{24,16},{32,40},{40,32},{48,56},{56,48},{1,9},... | collective-permute-start | bytes 98312 | tf_op jit(solution)/shard_map/ppermute | solution.py:280
  33.3 2.1 %collective-permute-done.3 = f32[16,512]{1,0:T(8,128)S(1)} collective-permute-done((f32[16,512]{1,0:T(8,128)S(1)}, f32[16,512]{1,0:T(8,128)S(1)}, u32[]{:S(2)}, u32[]{:S(2)}) %collective-permute-start.3) | collective-permute-done | bytes 32800 | tf_op jit(solution)/shard_map/ppermute | solution.py:280
  35.5 1.4 %all-to-all-done.parts = bf16[4,32,512]{2,1,0:T(8,128)(2,1)S(1)} async-done(((bf16[4,32,512]{2,1,0:T(8,128)(2,1)}), bf16[4,32,512]{2,1,0:T(8,128)(2,1)S(1)}, u32[]{:S(2)}, u32[]{:S(2)}) %all-to-all-start) | async-done | bytes 131104 | tf_op jit(solution)/shard_map/all_to_all | solution.py:372
  36.9 4.0 %contract.1 = bf16[8,112,256]{2,1,0:T(8,128)(2,1)} custom-call(s32[1,18]{1,0:T(1,128)S(1)} %get-tuple-element.25.info, bf16[4,32,512]{2,1,0:T(8,128)(2,1)S(1)} %all-to-all-done.parts, bf16[64,2048]{1,0:T(8,128)(2,1)S(1)} %collective-permute-done.ahead, bf16[1,512,2048]{2,1,0:T(8,128)(2,1)} %saved.3, bf16[1,512,2048]{2,1,0:T(8,128)(2,1)} %grads.3), custom_call_target="tpu_custom_call" | custom-call | flops 201326592 | bytes 4194304 | tf_op jit(solution)/shard_map/contract/pallas_call | solution.py:376
  40.9 4.2 %all-to-all-start.1 = ((bf16[8,112,256]{2,1,0:T(8,128)(2,1)}), bf16[8,112,256]{2,1,0:T(8,128)(2,1)S(1)}, u32[]{:S(2)}, u32[]{:S(2)}) async-start(bf16[8,112,256]{2,1,0:T(8,128)(2,1)} %contract.1), calls=%async_computation.1 | async-start | bytes 917504 | tf_op jit(solution)/shard_map/all_to_all | solution.py:391
  45.1 1.5 %collective-permute-start.4 = (f32[16,512]{1,0:T(8,128)S(1)}, f32[16,512]{1,0:T(8,128)S(1)}, u32[]{:S(2)}, u32[]{:S(2)}) collective-permute-start(f32[16,512]{1,0:T(8,128)S(1)} %add.17), channel_id=1, source_target_pairs={{0,16},{8,24},{16,0},{24,8},{32,48},{40,56},{48,32},{56,40},{1,17}... | collective-permute-start | bytes 98312 | tf_op jit(solution)/shard_map/ppermute | solution.py:280
  46.6 2.2 %collective-permute-done.4 = f32[16,512]{1,0:T(8,128)S(1)} collective-permute-done((f32[16,512]{1,0:T(8,128)S(1)}, f32[16,512]{1,0:T(8,128)S(1)}, u32[]{:S(2)}, u32[]{:S(2)}) %collective-permute-start.4) | collective-permute-done | bytes 32800 | tf_op jit(solution)/shard_map/ppermute | solution.py:280
  48.8 3.2 %all-to-all-done.1.pieces = bf16[8,112,256]{2,1,0:T(8,128)(2,1)S(1)} async-done(((bf16[8,112,256]{2,1,0:T(8,128)(2,1)}), bf16[8,112,256]{2,1,0:T(8,128)(2,1)S(1)}, u32[]{:S(2)}, u32[]{:S(2)}) %all-to-all-start.1) | async-done | bytes 458784 | tf_op jit(solution)/shard_map/all_to_all | solution.py:391
  52.0 0.5 collect_up.1
  52.5 3.4 %collective-permute-start.5 = (bf16[128,256]{1,0:T(8,128)(2,1)S(1)}, bf16[128,256]{1,0:T(8,128)(2,1)S(1)}, u32[]{:S(2)}, u32[]{:S(2)}) collective-permute-start(bf16[128,256]{1,0:T(8,128)(2,1)S(1)} %collect_up.1), channel_id=1, source_target_pairs={{0,192},{64,0},{128,64},{192,128},{1,193},{65,1},{129,65},{193,129... | collective-permute-start | bytes 196616 | tf_op jit(solution)/shard_map/ppermute | solution.py:275
  55.9 1.4 %collect_down.1.half = bf16[8,256,256]{2,1,0:T(8,128)(2,1)} custom-call(bf16[8,112,256]{2,1,0:T(8,128)(2,1)S(1)} %all-to-all-done.1.pieces), custom_call_target="tpu_custom_call" | custom-call | flops 1572864 | bytes 1048576 | tf_op jit(solution)/shard_map/collect_down/pallas_call | solution.py:406
  57.2 2.2 %collective-permute-done.5.block = bf16[128,256]{1,0:T(8,128)(2,1)S(1)} collective-permute-done((bf16[128,256]{1,0:T(8,128)(2,1)S(1)}, bf16[128,256]{1,0:T(8,128)(2,1)S(1)}, u32[]{:S(2)}, u32[]{:S(2)}) %collective-permute-start.5) | collective-permute-done | bytes 65568 | tf_op jit(solution)/shard_map/ppermute | solution.py:275
  59.4 0.9 %add_up.1 = bf16[8,256,256]{2,1,0:T(8,128)(2,1)} custom-call(bf16[128,256]{1,0:T(8,128)(2,1)S(1)} %collective-permute-done.5.block, bf16[8,256,256]{2,1,0:T(8,128)(2,1)} %collect_down.1.half), custom_call_target="tpu_custom_call", output_to_operand_aliasing={{}: (1, {})} | custom-call | bytes 524288 | tf_op jit(solution)/shard_map/add_up/pallas_call | solution.py:416
  60.3 3.6 %all-to-all-start.2 = ((bf16[8,256,256]{2,1,0:T(8,128)(2,1)}), bf16[8,256,256]{2,1,0:T(8,128)(2,1)S(1)}, u32[]{:S(2)}, u32[]{:S(2)}) async-start(bf16[8,256,256]{2,1,0:T(8,128)(2,1)} %add_up.1), calls=%async_computation.2 | async-start | bytes 2097152 | tf_op jit(solution)/shard_map/all_to_all | solution.py:429
  63.9 4.9 %collective-permute-start.7 = (f32[16,512]{1,0:T(8,128)S(1)}, f32[16,512]{1,0:T(8,128)S(1)}, u32[]{:S(2)}, u32[]{:S(2)}) collective-permute-start(f32[16,512]{1,0:T(8,128)S(1)} %add.18), channel_id=1, source_target_pairs={{0,32},{8,40},{16,48},{24,56},{32,0},{40,8},{48,16},{56,24},{1,33}... | collective-permute-start | bytes 98312 | tf_op jit(solution)/shard_map/ppermute | solution.py:280
  68.8 1.8 %collective-permute-done.7 = f32[16,512]{1,0:T(8,128)S(1)} collective-permute-done((f32[16,512]{1,0:T(8,128)S(1)}, f32[16,512]{1,0:T(8,128)S(1)}, u32[]{:S(2)}, u32[]{:S(2)}) %collective-permute-start.7) | collective-permute-done | bytes 32800 | tf_op jit(solution)/shard_map/ppermute | solution.py:280
  70.7 1.0 %copy-done.3 = bf16[1,8,16,2048]{3,2,1,0:T(8,128)(2,1)S(1)} copy-done((bf16[1,8,16,2048]{3,2,1,0:T(8,128)(2,1)S(1)}, bf16[1,8,16,2048]{3,2,1,0:T(8,128)(2,1)}, u32[]{:S(2)}) %copy-start.3) | copy-done | bytes 524312
  71.7 3.1 %hand_on.1 = bf16[1,512,2048]{2,1,0:T(8,128)(2,1)} custom-call(s32[1,18]{1,0:T(1,128)S(1)} %get-tuple-element.25.info, bf16[1,512,2048]{2,1,0:T(8,128)(2,1)S(1)} %collective-permute-done.6.arrived, f32[16,512]{1,0:T(8,128)S(1)} %add.19.fwd, bf16[1,8,16,2048]{3,2,1,0:T(8,128)(2,1)S(1)} %copy-done.3), custom_call_target="tpu_custom_call" | custom-call | flops 100663296 | bytes 4194304 | tf_op jit(solution)/shard_map/hand_on/pallas_call | solution.py:432
  74.9 2.8 %all-to-all-done.2.sums = bf16[8,256,256]{2,1,0:T(8,128)(2,1)S(1)} async-done(((bf16[8,256,256]{2,1,0:T(8,128)(2,1)}), bf16[8,256,256]{2,1,0:T(8,128)(2,1)S(1)}, u32[]{:S(2)}, u32[]{:S(2)}) %all-to-all-start.2) | async-done | bytes 1048608 | tf_op jit(solution)/shard_map/all_to_all | solution.py:429
  77.7 1.1 %unpack.1 = (bf16[1,8,16,2048]{3,2,1,0:T(8,128)(2,1)}, bf16[1,8,16,2048]{3,2,1,0:T(8,128)(2,1)}) custom-call(bf16[8,256,256]{2,1,0:T(8,128)(2,1)S(1)} %all-to-all-done.2.sums), custom_call_target="tpu_custom_call" | custom-call | bytes 2097152 | tf_op jit(solution)/shard_map/unpack/pallas_call | solution.py:444
  (19 shorter events, 0.1 us)
Async XLA Ops:
  0.6 7.1 %copy-start.2 = (bf16[1,8,16,2048]{3,2,1,0:T(8,128)(2,1)S(1)}, bf16[1,8,16,2048]{3,2,1,0:T(8,128)(2,1)}, u32[]{:S(2)}) copy-start(bf16[1,8,16,2048]{3,2,1,0:T(8,128)(2,1)} %down.5) | copy-start | bytes 1572868
  0.6 7.1 %copy-start.4 = (bf16[1,2,512,128]{3,2,1,0:T(8,128)(2,1)S(1)}, bf16[1,2,512,128]{3,2,1,0:T(8,128)(2,1)}, u32[]{:S(2)}) copy-start(bf16[1,2,512,128]{3,2,1,0:T(8,128)(2,1)} %keys_values.3) | copy-start | bytes 786436
  0.7 7.1 %copy-start = (bf16[1,512,2048]{2,1,0:T(8,128)(2,1)S(1)}, bf16[1,512,2048]{2,1,0:T(8,128)(2,1)}, u32[]{:S(2)}) copy-start(bf16[1,512,2048]{2,1,0:T(8,128)(2,1)} %queries.2) | copy-start | bytes 6291460
  3.5 7.7 %copy-start.1 = (bf16[1,512,2048]{2,1,0:T(8,128)(2,1)S(1)}, bf16[1,512,2048]{2,1,0:T(8,128)(2,1)}, u32[]{:S(2)}) copy-start(bf16[1,512,2048]{2,1,0:T(8,128)(2,1)} %grads.3) | copy-start | bytes 6291460
  3.5 7.6 %collective-permute-start = (bf16[64,2048]{1,0:T(8,128)(2,1)S(1)}, bf16[64,2048]{1,0:T(8,128)(2,1)S(1)}, u32[]{:S(2)}, u32[]{:S(2)}) collective-permute-start(bf16[64,2048]{1,0:T(8,128)(2,1)S(1)} %get-tuple-element.26), channel_id=1, source_target_pairs={{0,64},{64,128},{128,192},{192,0},{1,65},{65,129},{129,193},{193,1... | collective-permute-start | bytes 786440 | tf_op jit(solution)/shard_map/ppermute | solution.py:275
  11.9 5.5 %collective-permute-start.1 = (f32[16,512]{1,0:T(8,128)S(1)}, f32[16,512]{1,0:T(8,128)S(1)}, u32[]{:S(2)}, u32[]{:S(2)}) collective-permute-start(f32[16,512]{1,0:T(8,128)S(1)} %back_gradient.1), channel_id=1, source_target_pairs={{0,192},{64,0},{128,64},{192,128},{1,193},{65,1},{129,65},{193,129... | collective-permute-start | bytes 98312 | tf_op jit(solution)/shard_map/ppermute | solution.py:275
  17.4 42.9 %collective-permute-start.6 = (bf16[1,512,2048]{2,1,0:T(8,128)(2,1)}, bf16[1,512,2048]{2,1,0:T(8,128)(2,1)S(1)}, u32[]{:S(2)}, u32[]{:S(2)}) collective-permute-start(bf16[1,512,2048]{2,1,0:T(8,128)(2,1)} %param.11), channel_id=1, source_target_pairs={{0,64},{64,128},{128,192},{192,0},{1,65},{65,129},{129,193},{193,1... | collective-permute-start | bytes 6291464 | tf_op jit(solution)/shard_map/ppermute | solution.py:275
  17.4 10.4 %collective-permute-start.2 = (f32[32,512]{1,0:T(8,128)S(1)}, f32[32,512]{1,0:T(8,128)S(1)}, u32[]{:S(2)}, u32[]{:S(2)}) collective-permute-start(f32[32,512]{1,0:T(8,128)S(1)} %pad_maximum_fusion), channel_id=1, source_target_pairs={{0,32},{8,40},{16,48},{24,56},{32,0},{40,8},{48,16},{56,24},{1,33}... | collective-permute-start | bytes 196616 | tf_op jit(solution)/shard_map/ppermute | solution.py:280
  28.6 8.4 %all-to-all-start = ((bf16[4,32,512]{2,1,0:T(8,128)(2,1)}), bf16[4,32,512]{2,1,0:T(8,128)(2,1)S(1)}, u32[]{:S(2)}, u32[]{:S(2)}) async-start(bf16[4,32,512]{2,1,0:T(8,128)(2,1)} %broadcast_in_dim.2), calls=%async_computation | async-start | bytes 262144 | tf_op jit(solution)/shard_map/all_to_all | solution.py:372
  31.9 3.6 %collective-permute-start.3 = (f32[16,512]{1,0:T(8,128)S(1)}, f32[16,512]{1,0:T(8,128)S(1)}, u32[]{:S(2)}, u32[]{:S(2)}) collective-permute-start(f32[16,512]{1,0:T(8,128)S(1)} %constant_dynamic-update-slice_fusion), channel_id=1, source_target_pairs={{0,8},{8,0},{16,24},{24,16},{32,40},{40,32},{48,56},{56,48},{1,9},... | collective-permute-start | bytes 98312 | tf_op jit(solution)/shard_map/ppermute | solution.py:280
  40.9 11.1 %all-to-all-start.1 = ((bf16[8,112,256]{2,1,0:T(8,128)(2,1)}), bf16[8,112,256]{2,1,0:T(8,128)(2,1)S(1)}, u32[]{:S(2)}, u32[]{:S(2)}) async-start(bf16[8,112,256]{2,1,0:T(8,128)(2,1)} %contract.1), calls=%async_computation.1 | async-start | bytes 917504 | tf_op jit(solution)/shard_map/all_to_all | solution.py:391
  45.1 3.7 %collective-permute-start.4 = (f32[16,512]{1,0:T(8,128)S(1)}, f32[16,512]{1,0:T(8,128)S(1)}, u32[]{:S(2)}, u32[]{:S(2)}) collective-permute-start(f32[16,512]{1,0:T(8,128)S(1)} %add.17), channel_id=1, source_target_pairs={{0,16},{8,24},{16,0},{24,8},{32,48},{40,56},{48,32},{56,40},{1,17}... | collective-permute-start | bytes 98312 | tf_op jit(solution)/shard_map/ppermute | solution.py:280
  52.5 6.9 %collective-permute-start.5 = (bf16[128,256]{1,0:T(8,128)(2,1)S(1)}, bf16[128,256]{1,0:T(8,128)(2,1)S(1)}, u32[]{:S(2)}, u32[]{:S(2)}) collective-permute-start(bf16[128,256]{1,0:T(8,128)(2,1)S(1)} %collect_up.1), channel_id=1, source_target_pairs={{0,192},{64,0},{128,64},{192,128},{1,193},{65,1},{129,65},{193,129... | collective-permute-start | bytes 196616 | tf_op jit(solution)/shard_map/ppermute | solution.py:275
  60.3 17.4 %all-to-all-start.2 = ((bf16[8,256,256]{2,1,0:T(8,128)(2,1)}), bf16[8,256,256]{2,1,0:T(8,128)(2,1)S(1)}, u32[]{:S(2)}, u32[]{:S(2)}) async-start(bf16[8,256,256]{2,1,0:T(8,128)(2,1)} %add_up.1), calls=%async_computation.2 | async-start | bytes 2097152 | tf_op jit(solution)/shard_map/all_to_all | solution.py:429
  63.9 6.8 %collective-permute-start.7 = (f32[16,512]{1,0:T(8,128)S(1)}, f32[16,512]{1,0:T(8,128)S(1)}, u32[]{:S(2)}, u32[]{:S(2)}) collective-permute-start(f32[16,512]{1,0:T(8,128)S(1)} %add.18), channel_id=1, source_target_pairs={{0,32},{8,40},{16,48},{24,56},{32,0},{40,8},{48,16},{56,24},{1,33}... | collective-permute-start | bytes 98312 | tf_op jit(solution)/shard_map/ppermute | solution.py:280
  70.7 1.0 %copy-start.3 = (bf16[1,8,16,2048]{3,2,1,0:T(8,128)(2,1)S(1)}, bf16[1,8,16,2048]{3,2,1,0:T(8,128)(2,1)}, u32[]{:S(2)}) copy-start(bf16[1,8,16,2048]{3,2,1,0:T(8,128)(2,1)} %up.3) | copy-start | bytes 1572868

commit v4 on v3

--- a/solution.py
+++ b/solution.py
@@ -116,11 +116,11 @@
     out[...] = fold(full, note_masks(ahead, wide, length), rank)
 
 
-def attend_blocks(info, queries, keys_values, attended, first, last, base):
+def attend_blocks(info, queries, keys_values, attended):
     heads = queries.shape[2] // HD
     starts, lives, _ = recall(info, 0)
     power = math.log2(math.e) / math.sqrt(HD)
-    for j in range(first, last):
+    for j in range(attended.shape[0] // BLOCK):
         low, high = max(0, j + 1 - MOST_BLOCKS) * BLOCK, (j + 1) * BLOCK
         here = slice(j * BLOCK, high)
         start, live = starts[0], lives[0]
@@ -138,35 +138,25 @@
         scores = rows_by_rows(stacked, keys_values[0, 0, low:high, :])
         scores = jnp.where(seen, scores.reshape(heads, BLOCK, high - low), -1e30)
         top = jnp.max(scores, axis=-1, keepdims=True)
-        exponent = jnp.exp2((scores - top) * power)
-        total = jnp.sum(exponent, axis=-1, keepdims=True)
-        weights = (exponent * jnp.where(alive, 1.0 / total, 0.0)).astype(BF16)
+        exponent = jnp.exp2((scores - top) * power).astype(BF16)
+        values = jnp.concatenate(
+            [keys_values[0, 1, low:high, :], jnp.ones((high - low, HD), BF16)], axis=1
+        )
         mixed = jnp.dot(
-            weights.reshape(heads * BLOCK, high - low),
-            keys_values[0, 1, low:high, :],
-            preferred_element_type=F32,
-        ).astype(BF16)
+            exponent.reshape(heads * BLOCK, high - low), values, preferred_element_type=F32
+        ).reshape(heads, BLOCK, 2 * HD)
+        mixed = mixed[:, :, :HD] * jnp.where(alive, 1.0 / mixed[:, :, HD:], 0.0)
+        mixed = mixed.astype(BF16).reshape(heads * BLOCK, HD)
         for h in range(heads):
-            at = slice((j - base) * BLOCK, (j + 1 - base) * BLOCK)
-            attended[at, HD * h : HD * (h + 1)] = mixed[BLOCK * h : BLOCK * (h + 1)]
-
-
-def ranked_attention(info, down, attended, first, out):
+            attended[here, HD * h : HD * (h + 1)] = mixed[BLOCK * h : BLOCK * (h + 1)]
+
+
+def attention_kernel(info, queries, keys_values, down, out, attended):
+    attend_blocks(info, queries, keys_values, attended)
     rank, length = out.shape
     starts, lives, slots = recall(info, 0)
     full = rows_by_rows(pick_rows(down, slots), attended[...])
-    out[...] = fold(full, alive_rows(starts, lives, first, length), rank)
-
-
-def early_attention_kernel(info, queries, keys_values, down, out, attended):
-    attend_blocks(info, queries, keys_values, attended, 0, attended.shape[0] // BLOCK, 0)
-    ranked_attention(info, down, attended, 0, out)
-
-
-def late_attention_kernel(info, queries, keys_values, down, out, attended):
-    half = attended.shape[0] // BLOCK
-    attend_blocks(info, queries, keys_values, attended, half, 2 * half, half)
-    ranked_attention(info, down, attended, half * BLOCK, out)
+    out[...] = fold(full, alive_rows(starts, lives, 0, length), rank)
 
 
 def contract_kernel(info, parts, ahead, saved, grads, out, held, sems):
@@ -321,23 +311,21 @@
     )(*[in_hbm(x) for x in (*scalars, saved_attn, down_adapt, up_adapt)])
     theirs = shift(ahead, 1)
 
-    attention_cost = cost(
-        2 * length * MOST_BLOCKS * BLOCK * width + wide * length * width,
-        piece * 3 // 4,
-        length * MOST_BLOCKS * BLOCK * width // HD // 2,
-    )
-    half = length // 2
-    early = pl.pallas_call(
-        early_attention_kernel,
-        out_shape=pltpu.VMEM((rank, half), F32),
+    fwd_sum = pl.pallas_call(
+        attention_kernel,
+        out_shape=pltpu.VMEM((rank, length), F32),
         in_specs=[SMEM] + [VMEM] * 3,
         out_specs=VMEM,
-        scratch_shapes=[pltpu.VMEM((half, width), BF16)],
-        compiler_params=PARAMS,
-        cost_estimate=attention_cost,
-        name="early_attention",
+        scratch_shapes=[pltpu.VMEM((length, width), BF16)],
+        compiler_params=PARAMS,
+        cost_estimate=cost(
+            4 * length * MOST_BLOCKS * BLOCK * width + 2 * wide * length * width,
+            piece * 3 // 2,
+            length * MOST_BLOCKS * BLOCK * width // HD,
+        ),
+        name="attention",
     )(info, queries, keys_values, down_adapt)
-    theirs, early = lax.optimization_barrier((theirs, early))
+    theirs, fwd_sum = lax.optimization_barrier((theirs, fwd_sum))
 
     grad_part = pl.pallas_call(
         back_gradient_kernel,
@@ -355,23 +343,12 @@
 
     back = theirs[wide:, length : 2 * length].astype(F32) + theirs[wide:, 2 * length : 3 * length].astype(F32)
     parts = jnp.concatenate([back, grad_part], axis=0)
-    queries, act_inbox, parts = lax.optimization_barrier((queries, act_inbox, parts))
+    act_inbox, fwd_sum, parts = lax.optimization_barrier((act_inbox, fwd_sum, parts))
     parts = exchange_add(parts, 4).astype(BF16)
     arrived = shift(act_inbox, 1)
-    late = pl.pallas_call(
-        late_attention_kernel,
-        out_shape=pltpu.VMEM((rank, half), F32),
-        in_specs=[SMEM] + [VMEM] * 3,
-        out_specs=VMEM,
-        scratch_shapes=[pltpu.VMEM((half, width), BF16)],
-        compiler_params=PARAMS,
-        cost_estimate=attention_cost,
-        name="late_attention",
-    )(info, queries, keys_values, down_adapt)
-    parts, late = lax.optimization_barrier((parts, late))
+    parts, fwd_sum = lax.optimization_barrier((parts, fwd_sum))
     parts = lax.all_to_all(copies(parts, lax.axis_size("zi")), "zi", 0, 0)
-
-    fwd_sum = exchange_add(jnp.concatenate([early, late], axis=1), 1)
+    fwd_sum = exchange_add(fwd_sum, 1)
 
     pieces = pl.pallas_call(
         contract_kernel,
@@ -387,8 +364,8 @@
         name="contract",
     )(info, parts, theirs, in_hbm(saved_attn), in_hbm(grad_inbox))
     pieces, fwd_sum = lax.optimization_barrier((pieces, fwd_sum))
+    pieces = lax.all_to_all(pieces, "dp", 0, 0)
     fwd_sum = exchange_add(fwd_sum, 2)
-    pieces = lax.all_to_all(pieces, "dp", 0, 0)
     pieces, fwd_sum = lax.optimization_barrier((pieces, fwd_sum))
 
     rows = slot_count * rank

time: 79.1 us -> 79 us (level)
  Pallas kernels: 21.3 us -> 18.2 us
  waiting for transfers between devices: 18.3 us -> 20.4 us
  starting transfers between devices: 36.5 us -> 37.5 us
    pallas_call x2 -> x1, Pallas kernels: 6.84 us -> 3.67 us  [per_device(): pl.pallas_call(attention_kernel, out_shape=pltpu.VMEM((rank, length), F32...]
    ppermute x4, waiting for transfers between devices: 6.18 us -> 8.25 us  [exchange_add(): lax.ppermute(value, TENSOR, [(i, i ^ distance) for i in range(count)])]
  transfers between devices with their start and end apart: 11 -> 11, of which waited for: 8 -> 9; matrix products, arithmetic and copies ran while one was open for 1% -> 1% of each run, Pallas kernels for 21% -> 17%
where the time goes in v4:
time: 79 us; the launch traced here: 78.6 us
  starting transfers between devices  37.5 us (47%)
  waiting for transfers between devices  20.4 us (26%)
  Pallas kernels  18.2 us (23%)
  local copies, waits for them, and re-layouts  1.72 us (2%)
    ppermute x4, starting transfers between devices, exchange_add(): lax.ppermute(value, TENSOR, [(i, i ^ distance) for i in range(count)])  14.9 us
    ppermute x4, starting transfers between devices, shift(): lax.ppermute(value, 'section', [(i, (i + steps) % count) for i in range(c...  11.2 us
    ppermute x4, waiting for transfers between devices, exchange_add(): lax.ppermute(value, TENSOR, [(i, i ^ distance) for i in range(count)])  8.25 us
    ppermute x4, waiting for transfers between devices, shift(): lax.ppermute(value, 'section', [(i, (i + steps) % count) for i in range(c...  4.69 us
    all_to_all x1, starting transfers between devices, per_device(): pieces = lax.all_to_all(pieces, 'dp', 0, 0)  4.2 us
    pallas_call x1, Pallas kernels, per_device(): pl.pallas_call(contract_kernel, out_shape=jax.ShapeDtypeStruct((dp_count,...  4 us
    pallas_call x1, Pallas kernels, per_device(): pl.pallas_call(attention_kernel, out_shape=pltpu.VMEM((rank, length), F32...  3.67 us
    all_to_all x1, starting transfers between devices, per_device(): parts = lax.all_to_all(copies(parts, lax.axis_size('zi')), 'zi', 0, 0)  3.6 us
  transfers between devices with their start and end apart: 11, of which 9 were waited for; matrix products, arithmetic and copies ran while one was open for 1% of the time, Pallas kernels for 17%

profile of v4, /device:TPU:1, one launch (start us, length us, event | category | flops | bytes accessed | tf_op | source)
XLA Modules:
  0.0 78.6 jit_solution(1691878604137751050)
XLA Ops:
  0.7 2.8 %prepare.1 = (bf16[64,2048]{1,0:T(8,128)(2,1)S(1)}, s32[1,18]{1,0:T(1,128)S(1)}) custom-call(s32[1,2,1,3]{3,2,1,0:T(1,128)} %blocks.1, s32[1,2,1,3]{3,2,1,0:T(1,128)} %pads.1, s32[1,2,1,3]{3,2,1,0:T(1,128)} %tenants.1, s32[32]{0:T(128)} %table.1, bf16[1,512,2048]{2,1,0:T(8,128)(2,1)} %saved.3, bf16[1,8,16,2048]{3,2,1,0:T(8,128)(2,1)} %down.3, ...), custom_call_target="tpu_custom_call" | custom-call | flops 100663296 | bytes 10485760 | tf_op jit(solution)/shard_map/prepare/pallas_call | solution.py:295
  3.5 4.2 %collective-permute-start = (bf16[64,2048]{1,0:T(8,128)(2,1)S(1)}, bf16[64,2048]{1,0:T(8,128)(2,1)S(1)}, u32[]{:S(2)}, u32[]{:S(2)}) collective-permute-start(bf16[64,2048]{1,0:T(8,128)(2,1)S(1)} %get-tuple-element.26), channel_id=1, source_target_pairs={{0,64},{64,128},{128,192},{192,0},{1,65},{65,129},{129,193},{193,1... | collective-permute-start | bytes 786440 | tf_op jit(solution)/shard_map/ppermute | solution.py:265
  7.7 3.7 %attention.1 = f32[16,512]{1,0:T(8,128)S(1)} custom-call(s32[1,18]{1,0:T(1,128)S(1)} %get-tuple-element.25.info, bf16[1,512,2048]{2,1,0:T(8,128)(2,1)S(1)} %copy-done.3, bf16[1,2,512,128]{3,2,1,0:T(8,128)(2,1)S(1)} %copy-done.4, bf16[1,8,16,2048]{3,2,1,0:T(8,128)(2,1)S(1)} %copy-done.2), custom_call_target="tpu_custom_call" | custom-call | flops 1174405120 | bytes 3145728 | tf_op jit(solution)/shard_map/attention/pallas_call | solution.py:314
  11.4 0.0 collective-permute-done.ahead
  11.4 0.7 back_gradient.1
  12.2 2.8 %collective-permute-start.1 = (f32[16,512]{1,0:T(8,128)S(1)}, f32[16,512]{1,0:T(8,128)S(1)}, u32[]{:S(2)}, u32[]{:S(2)}) collective-permute-start(f32[16,512]{1,0:T(8,128)S(1)} %back_gradient.1), channel_id=1, source_target_pairs={{0,192},{64,0},{128,64},{192,128},{1,193},{65,1},{129,65},{193,129... | collective-permute-start | bytes 98312 | tf_op jit(solution)/shard_map/ppermute | solution.py:265
  14.9 2.5 %collective-permute-done.1 = f32[16,512]{1,0:T(8,128)S(1)} collective-permute-done((f32[16,512]{1,0:T(8,128)S(1)}, f32[16,512]{1,0:T(8,128)S(1)}, u32[]{:S(2)}, u32[]{:S(2)}) %collective-permute-start.1) | collective-permute-done | bytes 32800 | tf_op jit(solution)/shard_map/ppermute | solution.py:265
  17.4 0.0 collective-permute-start.6
  17.4 7.0 %collective-permute-start.2 = (f32[32,512]{1,0:T(8,128)S(1)}, f32[32,512]{1,0:T(8,128)S(1)}, u32[]{:S(2)}, u32[]{:S(2)}) collective-permute-start(f32[32,512]{1,0:T(8,128)S(1)} %pad_maximum_fusion), channel_id=1, source_target_pairs={{0,32},{8,40},{16,48},{24,56},{32,0},{40,8},{48,16},{56,24},{1,33}... | collective-permute-start | bytes 196616 | tf_op jit(solution)/shard_map/ppermute | solution.py:270
  24.4 2.1 %collective-permute-done.2 = f32[32,512]{1,0:T(8,128)S(1)} collective-permute-done((f32[32,512]{1,0:T(8,128)S(1)}, f32[32,512]{1,0:T(8,128)S(1)}, u32[]{:S(2)}, u32[]{:S(2)}) %collective-permute-start.2) | collective-permute-done | bytes 65568 | tf_op jit(solution)/shard_map/ppermute | solution.py:270
  26.6 0.7 broadcast_in_dim.2
  27.2 3.6 %all-to-all-start = ((bf16[4,32,512]{2,1,0:T(8,128)(2,1)}), bf16[4,32,512]{2,1,0:T(8,128)(2,1)S(1)}, u32[]{:S(2)}, u32[]{:S(2)}) async-start(bf16[4,32,512]{2,1,0:T(8,128)(2,1)} %broadcast_in_dim.2), calls=%async_computation | async-start | bytes 262144 | tf_op jit(solution)/shard_map/all_to_all | solution.py:350
  30.8 1.5 %collective-permute-start.3 = (f32[16,512]{1,0:T(8,128)S(1)}, f32[16,512]{1,0:T(8,128)S(1)}, u32[]{:S(2)}, u32[]{:S(2)}) collective-permute-start(f32[16,512]{1,0:T(8,128)S(1)} %attention.1), channel_id=1, source_target_pairs={{0,8},{8,0},{16,24},{24,16},{32,40},{40,32},{48,56},{56,48},{1,9},... | collective-permute-start | bytes 98312 | tf_op jit(solution)/shard_map/ppermute | solution.py:270
  32.3 2.2 %collective-permute-done.3 = f32[16,512]{1,0:T(8,128)S(1)} collective-permute-done((f32[16,512]{1,0:T(8,128)S(1)}, f32[16,512]{1,0:T(8,128)S(1)}, u32[]{:S(2)}, u32[]{:S(2)}) %collective-permute-start.3) | collective-permute-done | bytes 32800 | tf_op jit(solution)/shard_map/ppermute | solution.py:270
  34.5 1.4 %all-to-all-done.parts = bf16[4,32,512]{2,1,0:T(8,128)(2,1)S(1)} async-done(((bf16[4,32,512]{2,1,0:T(8,128)(2,1)}), bf16[4,32,512]{2,1,0:T(8,128)(2,1)S(1)}, u32[]{:S(2)}, u32[]{:S(2)}) %all-to-all-start) | async-done | bytes 131104 | tf_op jit(solution)/shard_map/all_to_all | solution.py:350
  35.9 4.0 %contract.1 = bf16[8,112,256]{2,1,0:T(8,128)(2,1)} custom-call(s32[1,18]{1,0:T(1,128)S(1)} %get-tuple-element.25.info, bf16[4,32,512]{2,1,0:T(8,128)(2,1)S(1)} %all-to-all-done.parts, bf16[64,2048]{1,0:T(8,128)(2,1)S(1)} %collective-permute-done.ahead, bf16[1,512,2048]{2,1,0:T(8,128)(2,1)} %saved.3, bf16[1,512,2048]{2,1,0:T(8,128)(2,1)} %grads.3), custom_call_target="tpu_custom_call" | custom-call | flops 201326592 | bytes 4194304 | tf_op jit(solution)/shard_map/contract/pallas_call | solution.py:353
  39.9 4.2 %all-to-all-start.1 = ((bf16[8,112,256]{2,1,0:T(8,128)(2,1)}), bf16[8,112,256]{2,1,0:T(8,128)(2,1)S(1)}, u32[]{:S(2)}, u32[]{:S(2)}) async-start(bf16[8,112,256]{2,1,0:T(8,128)(2,1)} %contract.1), calls=%async_computation.1 | async-start | bytes 917504 | tf_op jit(solution)/shard_map/all_to_all | solution.py:367
  44.1 1.4 %collective-permute-start.4 = (f32[16,512]{1,0:T(8,128)S(1)}, f32[16,512]{1,0:T(8,128)S(1)}, u32[]{:S(2)}, u32[]{:S(2)}) collective-permute-start(f32[16,512]{1,0:T(8,128)S(1)} %add.17), channel_id=1, source_target_pairs={{0,16},{8,24},{16,0},{24,8},{32,48},{40,56},{48,32},{56,40},{1,17}... | collective-permute-start | bytes 98312 | tf_op jit(solution)/shard_map/ppermute | solution.py:270
  45.5 2.3 %collective-permute-done.4 = f32[16,512]{1,0:T(8,128)S(1)} collective-permute-done((f32[16,512]{1,0:T(8,128)S(1)}, f32[16,512]{1,0:T(8,128)S(1)}, u32[]{:S(2)}, u32[]{:S(2)}) %collective-permute-start.4) | collective-permute-done | bytes 32800 | tf_op jit(solution)/shard_map/ppermute | solution.py:270
  47.8 3.2 %all-to-all-done.1.pieces = bf16[8,112,256]{2,1,0:T(8,128)(2,1)S(1)} async-done(((bf16[8,112,256]{2,1,0:T(8,128)(2,1)}), bf16[8,112,256]{2,1,0:T(8,128)(2,1)S(1)}, u32[]{:S(2)}, u32[]{:S(2)}) %all-to-all-start.1) | async-done | bytes 458784 | tf_op jit(solution)/shard_map/all_to_all | solution.py:367
  51.0 0.5 collect_up.1
  51.5 4.2 %collective-permute-start.5 = (bf16[128,256]{1,0:T(8,128)(2,1)S(1)}, bf16[128,256]{1,0:T(8,128)(2,1)S(1)}, u32[]{:S(2)}, u32[]{:S(2)}) collective-permute-start(bf16[128,256]{1,0:T(8,128)(2,1)S(1)} %collect_up.1), channel_id=1, source_target_pairs={{0,192},{64,0},{128,64},{192,128},{1,193},{65,1},{129,65},{193,129... | collective-permute-start | bytes 196616 | tf_op jit(solution)/shard_map/ppermute | solution.py:265
  55.7 1.4 %collect_down.1.half = bf16[8,256,256]{2,1,0:T(8,128)(2,1)} custom-call(bf16[8,112,256]{2,1,0:T(8,128)(2,1)S(1)} %all-to-all-done.1.pieces), custom_call_target="tpu_custom_call" | custom-call | flops 1572864 | bytes 1048576 | tf_op jit(solution)/shard_map/collect_down/pallas_call | solution.py:383
  57.1 2.2 %collective-permute-done.5.block = bf16[128,256]{1,0:T(8,128)(2,1)S(1)} collective-permute-done((bf16[128,256]{1,0:T(8,128)(2,1)S(1)}, bf16[128,256]{1,0:T(8,128)(2,1)S(1)}, u32[]{:S(2)}, u32[]{:S(2)}) %collective-permute-start.5) | collective-permute-done | bytes 65568 | tf_op jit(solution)/shard_map/ppermute | solution.py:265
  59.3 0.9 %add_up.1 = bf16[8,256,256]{2,1,0:T(8,128)(2,1)} custom-call(bf16[128,256]{1,0:T(8,128)(2,1)S(1)} %collective-permute-done.5.block, bf16[8,256,256]{2,1,0:T(8,128)(2,1)} %collect_down.1.half), custom_call_target="tpu_custom_call", output_to_operand_aliasing={{}: (1, {})} | custom-call | bytes 524288 | tf_op jit(solution)/shard_map/add_up/pallas_call | solution.py:393
  60.2 3.6 %all-to-all-start.2 = ((bf16[8,256,256]{2,1,0:T(8,128)(2,1)}), bf16[8,256,256]{2,1,0:T(8,128)(2,1)S(1)}, u32[]{:S(2)}, u32[]{:S(2)}) async-start(bf16[8,256,256]{2,1,0:T(8,128)(2,1)} %add_up.1), calls=%async_computation.2 | async-start | bytes 2097152 | tf_op jit(solution)/shard_map/all_to_all | solution.py:406
  63.7 5.1 %collective-permute-start.7 = (f32[16,512]{1,0:T(8,128)S(1)}, f32[16,512]{1,0:T(8,128)S(1)}, u32[]{:S(2)}, u32[]{:S(2)}) collective-permute-start(f32[16,512]{1,0:T(8,128)S(1)} %add.18), channel_id=1, source_target_pairs={{0,32},{8,40},{16,48},{24,56},{32,0},{40,8},{48,16},{56,24},{1,33}... | collective-permute-start | bytes 98312 | tf_op jit(solution)/shard_map/ppermute | solution.py:270
  68.8 1.7 %collective-permute-done.7 = f32[16,512]{1,0:T(8,128)S(1)} collective-permute-done((f32[16,512]{1,0:T(8,128)S(1)}, f32[16,512]{1,0:T(8,128)S(1)}, u32[]{:S(2)}, u32[]{:S(2)}) %collective-permute-start.7) | collective-permute-done | bytes 32800 | tf_op jit(solution)/shard_map/ppermute | solution.py:270
  70.5 1.0 %copy-done.1 = bf16[1,8,16,2048]{3,2,1,0:T(8,128)(2,1)S(1)} copy-done((bf16[1,8,16,2048]{3,2,1,0:T(8,128)(2,1)S(1)}, bf16[1,8,16,2048]{3,2,1,0:T(8,128)(2,1)}, u32[]{:S(2)}) %copy-start.1) | copy-done | bytes 524312
  71.6 3.1 %hand_on.1 = bf16[1,512,2048]{2,1,0:T(8,128)(2,1)} custom-call(s32[1,18]{1,0:T(1,128)S(1)} %get-tuple-element.25.info, bf16[1,512,2048]{2,1,0:T(8,128)(2,1)S(1)} %collective-permute-done.6.arrived, f32[16,512]{1,0:T(8,128)S(1)} %add.19.fwd, bf16[1,8,16,2048]{3,2,1,0:T(8,128)(2,1)S(1)} %copy-done.1), custom_call_target="tpu_custom_call" | custom-call | flops 100663296 | bytes 4194304 | tf_op jit(solution)/shard_map/hand_on/pallas_call | solution.py:409
  74.7 2.8 %all-to-all-done.2.sums = bf16[8,256,256]{2,1,0:T(8,128)(2,1)S(1)} async-done(((bf16[8,256,256]{2,1,0:T(8,128)(2,1)}), bf16[8,256,256]{2,1,0:T(8,128)(2,1)S(1)}, u32[]{:S(2)}, u32[]{:S(2)}) %all-to-all-start.2) | async-done | bytes 1048608 | tf_op jit(solution)/shard_map/all_to_all | solution.py:406
  77.5 1.1 %unpack.1 = (bf16[1,8,16,2048]{3,2,1,0:T(8,128)(2,1)}, bf16[1,8,16,2048]{3,2,1,0:T(8,128)(2,1)}) custom-call(bf16[8,256,256]{2,1,0:T(8,128)(2,1)S(1)} %all-to-all-done.2.sums), custom_call_target="tpu_custom_call" | custom-call | bytes 2097152 | tf_op jit(solution)/shard_map/unpack/pallas_call | solution.py:421
  (16 shorter events, 0.1 us)
Async XLA Ops:
  0.6 7.1 %copy-start.2 = (bf16[1,8,16,2048]{3,2,1,0:T(8,128)(2,1)S(1)}, bf16[1,8,16,2048]{3,2,1,0:T(8,128)(2,1)}, u32[]{:S(2)}) copy-start(bf16[1,8,16,2048]{3,2,1,0:T(8,128)(2,1)} %down.3) | copy-start | bytes 1572868
  0.6 7.1 %copy-start.4 = (bf16[1,2,512,128]{3,2,1,0:T(8,128)(2,1)S(1)}, bf16[1,2,512,128]{3,2,1,0:T(8,128)(2,1)}, u32[]{:S(2)}) copy-start(bf16[1,2,512,128]{3,2,1,0:T(8,128)(2,1)} %keys_values.1) | copy-start | bytes 786436
  0.7 7.0 %copy-start.3 = (bf16[1,512,2048]{2,1,0:T(8,128)(2,1)S(1)}, bf16[1,512,2048]{2,1,0:T(8,128)(2,1)}, u32[]{:S(2)}) copy-start(bf16[1,512,2048]{2,1,0:T(8,128)(2,1)} %queries.1) | copy-start | bytes 6291460
  3.5 7.9 %collective-permute-start = (bf16[64,2048]{1,0:T(8,128)(2,1)S(1)}, bf16[64,2048]{1,0:T(8,128)(2,1)S(1)}, u32[]{:S(2)}, u32[]{:S(2)}) collective-permute-start(bf16[64,2048]{1,0:T(8,128)(2,1)S(1)} %get-tuple-element.26), channel_id=1, source_target_pairs={{0,64},{64,128},{128,192},{192,0},{1,65},{65,129},{129,193},{193,1... | collective-permute-start | bytes 786440 | tf_op jit(solution)/shard_map/ppermute | solution.py:265
  7.7 3.7 %copy-start = (bf16[1,512,2048]{2,1,0:T(8,128)(2,1)S(1)}, bf16[1,512,2048]{2,1,0:T(8,128)(2,1)}, u32[]{:S(2)}) copy-start(bf16[1,512,2048]{2,1,0:T(8,128)(2,1)} %grads.3) | copy-start | bytes 6291460
  12.2 5.3 %collective-permute-start.1 = (f32[16,512]{1,0:T(8,128)S(1)}, f32[16,512]{1,0:T(8,128)S(1)}, u32[]{:S(2)}, u32[]{:S(2)}) collective-permute-start(f32[16,512]{1,0:T(8,128)S(1)} %back_gradient.1), channel_id=1, source_target_pairs={{0,192},{64,0},{128,64},{192,128},{1,193},{65,1},{129,65},{193,129... | collective-permute-start | bytes 98312 | tf_op jit(solution)/shard_map/ppermute | solution.py:265
  17.4 42.7 %collective-permute-start.6 = (bf16[1,512,2048]{2,1,0:T(8,128)(2,1)}, bf16[1,512,2048]{2,1,0:T(8,128)(2,1)S(1)}, u32[]{:S(2)}, u32[]{:S(2)}) collective-permute-start(bf16[1,512,2048]{2,1,0:T(8,128)(2,1)} %param.11), channel_id=1, source_target_pairs={{0,64},{64,128},{128,192},{192,0},{1,65},{65,129},{129,193},{193,1... | collective-permute-start | bytes 6291464 | tf_op jit(solution)/shard_map/ppermute | solution.py:265
  17.4 9.1 %collective-permute-start.2 = (f32[32,512]{1,0:T(8,128)S(1)}, f32[32,512]{1,0:T(8,128)S(1)}, u32[]{:S(2)}, u32[]{:S(2)}) collective-permute-start(f32[32,512]{1,0:T(8,128)S(1)} %pad_maximum_fusion), channel_id=1, source_target_pairs={{0,32},{8,40},{16,48},{24,56},{32,0},{40,8},{48,16},{56,24},{1,33}... | collective-permute-start | bytes 196616 | tf_op jit(solution)/shard_map/ppermute | solution.py:270
  27.2 8.7 %all-to-all-start = ((bf16[4,32,512]{2,1,0:T(8,128)(2,1)}), bf16[4,32,512]{2,1,0:T(8,128)(2,1)S(1)}, u32[]{:S(2)}, u32[]{:S(2)}) async-start(bf16[4,32,512]{2,1,0:T(8,128)(2,1)} %broadcast_in_dim.2), calls=%async_computation | async-start | bytes 262144 | tf_op jit(solution)/shard_map/all_to_all | solution.py:350
  30.8 3.6 %collective-permute-start.3 = (f32[16,512]{1,0:T(8,128)S(1)}, f32[16,512]{1,0:T(8,128)S(1)}, u32[]{:S(2)}, u32[]{:S(2)}) collective-permute-start(f32[16,512]{1,0:T(8,128)S(1)} %attention.1), channel_id=1, source_target_pairs={{0,8},{8,0},{16,24},{24,16},{32,40},{40,32},{48,56},{56,48},{1,9},... | collective-permute-start | bytes 98312 | tf_op jit(solution)/shard_map/ppermute | solution.py:270
  39.9 11.1 %all-to-all-start.1 = ((bf16[8,112,256]{2,1,0:T(8,128)(2,1)}), bf16[8,112,256]{2,1,0:T(8,128)(2,1)S(1)}, u32[]{:S(2)}, u32[]{:S(2)}) async-start(bf16[8,112,256]{2,1,0:T(8,128)(2,1)} %contract.1), calls=%async_computation.1 | async-start | bytes 917504 | tf_op jit(solution)/shard_map/all_to_all | solution.py:367
  44.1 3.7 %collective-permute-start.4 = (f32[16,512]{1,0:T(8,128)S(1)}, f32[16,512]{1,0:T(8,128)S(1)}, u32[]{:S(2)}, u32[]{:S(2)}) collective-permute-start(f32[16,512]{1,0:T(8,128)S(1)} %add.17), channel_id=1, source_target_pairs={{0,16},{8,24},{16,0},{24,8},{32,48},{40,56},{48,32},{56,40},{1,17}... | collective-permute-start | bytes 98312 | tf_op jit(solution)/shard_map/ppermute | solution.py:270
  51.5 7.8 %collective-permute-start.5 = (bf16[128,256]{1,0:T(8,128)(2,1)S(1)}, bf16[128,256]{1,0:T(8,128)(2,1)S(1)}, u32[]{:S(2)}, u32[]{:S(2)}) collective-permute-start(bf16[128,256]{1,0:T(8,128)(2,1)S(1)} %collect_up.1), channel_id=1, source_target_pairs={{0,192},{64,0},{128,64},{192,128},{1,193},{65,1},{129,65},{193,129... | collective-permute-start | bytes 196616 | tf_op jit(solution)/shard_map/ppermute | solution.py:265
  60.2 17.4 %all-to-all-start.2 = ((bf16[8,256,256]{2,1,0:T(8,128)(2,1)}), bf16[8,256,256]{2,1,0:T(8,128)(2,1)S(1)}, u32[]{:S(2)}, u32[]{:S(2)}) async-start(bf16[8,256,256]{2,1,0:T(8,128)(2,1)} %add_up.1), calls=%async_computation.2 | async-start | bytes 2097152 | tf_op jit(solution)/shard_map/all_to_all | solution.py:406
  63.7 6.8 %collective-permute-start.7 = (f32[16,512]{1,0:T(8,128)S(1)}, f32[16,512]{1,0:T(8,128)S(1)}, u32[]{:S(2)}, u32[]{:S(2)}) collective-permute-start(f32[16,512]{1,0:T(8,128)S(1)} %add.18), channel_id=1, source_target_pairs={{0,32},{8,40},{16,48},{24,56},{32,0},{40,8},{48,16},{56,24},{1,33}... | collective-permute-start | bytes 98312 | tf_op jit(solution)/shard_map/ppermute | solution.py:270
  70.5 1.0 %copy-start.1 = (bf16[1,8,16,2048]{3,2,1,0:T(8,128)(2,1)S(1)}, bf16[1,8,16,2048]{3,2,1,0:T(8,128)(2,1)}, u32[]{:S(2)}) copy-start(bf16[1,8,16,2048]{3,2,1,0:T(8,128)(2,1)} %up.3) | copy-start | bytes 1572868

commit v5 on v3

--- a/solution.py
+++ b/solution.py
@@ -337,7 +337,8 @@
         cost_estimate=attention_cost,
         name="early_attention",
     )(info, queries, keys_values, down_adapt)
-    theirs, early = lax.optimization_barrier((theirs, early))
+    theirs, early, act_inbox = lax.optimization_barrier((theirs, early, act_inbox))
+    arrived = shift(act_inbox, 1)
 
     grad_part = pl.pallas_call(
         back_gradient_kernel,
@@ -355,9 +356,8 @@
 
     back = theirs[wide:, length : 2 * length].astype(F32) + theirs[wide:, 2 * length : 3 * length].astype(F32)
     parts = jnp.concatenate([back, grad_part], axis=0)
-    queries, act_inbox, parts = lax.optimization_barrier((queries, act_inbox, parts))
+    queries, parts = lax.optimization_barrier((queries, parts))
     parts = exchange_add(parts, 4).astype(BF16)
-    arrived = shift(act_inbox, 1)
     late = pl.pallas_call(
         late_attention_kernel,
         out_shape=pltpu.VMEM((rank, half), F32),

time: 79.1 us -> 84 us (1.062)
  waiting for transfers between devices: 18.3 us -> 25.8 us
  starting transfers between devices: 36.5 us -> 33.6 us
  Pallas kernels: 21.3 us -> 22.6 us
  local copies, waits for them, and re-layouts: 1.73 us -> 0.7 us
    ppermute x4, waiting for transfers between devices: 4.69 us -> 8.88 us  [shift(): lax.ppermute(value, 'section', [(i, (i + steps) % count) for i in range(c...]
    ppermute x4, starting transfers between devices: 10.6 us -> 8.79 us  [shift(): lax.ppermute(value, 'section', [(i, (i + steps) % count) for i in range(c...]
    all_to_all x1, waiting for transfers between devices: 3.19 us -> 4.68 us  [per_device(): pieces = lax.all_to_all(pieces, 'dp', 0, 0)]
    ppermute x4, waiting for transfers between devices: 6.18 us -> 7.66 us  [exchange_add(): lax.ppermute(value, TENSOR, [(i, i ^ distance) for i in range(count)])]
    pallas_call x1, Pallas kernels: 3.13 us -> 4.39 us  [per_device(): pl.pallas_call(hand_on_kernel, grid=(length // rows,), out_shape=jax.Shap...]
    unnamed x11, local copies, waits for them, and re-layouts: 1.06 us -> 0.03 us
  transfers between devices with their start and end apart: 11 -> 11, of which waited for: 8 -> 8; matrix products, arithmetic and copies ran while one was open for 1% -> 1% of each run, Pallas kernels for 21% -> 22%
where the time goes in v5:
time: 84 us; the launch traced here: 83.6 us
  starting transfers between devices  33.6 us (40%)
  waiting for transfers between devices  25.8 us (31%)
  Pallas kernels  22.6 us (27%)
    ppermute x4, starting transfers between devices, exchange_add(): lax.ppermute(value, TENSOR, [(i, i ^ distance) for i in range(count)])  14 us
    ppermute x4, waiting for transfers between devices, shift(): lax.ppermute(value, 'section', [(i, (i + steps) % count) for i in range(c...  8.88 us
    ppermute x4, starting transfers between devices, shift(): lax.ppermute(value, 'section', [(i, (i + steps) % count) for i in range(c...  8.79 us
    ppermute x4, waiting for transfers between devices, exchange_add(): lax.ppermute(value, TENSOR, [(i, i ^ distance) for i in range(count)])  7.66 us
    all_to_all x1, waiting for transfers between devices, per_device(): pieces = lax.all_to_all(pieces, 'dp', 0, 0)  4.68 us
    pallas_call x1, Pallas kernels, per_device(): pl.pallas_call(hand_on_kernel, grid=(length // rows,), out_shape=jax.Shap...  4.39 us
    pallas_call x1, Pallas kernels, per_device(): pl.pallas_call(contract_kernel, out_shape=jax.ShapeDtypeStruct((dp_count,...  4 us
    all_to_all x1, starting transfers between devices, per_device(): pieces = lax.all_to_all(pieces, 'dp', 0, 0)  3.98 us
  transfers between devices with their start and end apart: 11, of which 8 were waited for; matrix products, arithmetic and copies ran while one was open for 1% of the time, Pallas kernels for 22%

profile of v5, /device:TPU:1, one launch (start us, length us, event | category | flops | bytes accessed | tf_op | source)
XLA Modules:
  0.0 83.6 jit_solution(10285815674299337281)
XLA Ops:
  0.7 2.8 %prepare.1 = (bf16[64,2048]{1,0:T(8,128)(2,1)S(1)}, s32[1,18]{1,0:T(1,128)S(1)}) custom-call(s32[1,2,1,3]{3,2,1,0:T(1,128)} %blocks.1, s32[1,2,1,3]{3,2,1,0:T(1,128)} %pads.1, s32[1,2,1,3]{3,2,1,0:T(1,128)} %tenants.1, s32[32]{0:T(128)} %table.1, bf16[1,512,2048]{2,1,0:T(8,128)(2,1)} %saved.3, bf16[1,8,16,2048]{3,2,1,0:T(8,128)(2,1)} %down.5, ...), custom_call_target="tpu_custom_call" | custom-call | flops 100663296 | bytes 10485760 | tf_op jit(solution)/shard_map/prepare/pallas_call | solution.py:305
  3.5 0.0 copy-start.1
  3.5 4.2 %collective-permute-start = (bf16[64,2048]{1,0:T(8,128)(2,1)S(1)}, bf16[64,2048]{1,0:T(8,128)(2,1)S(1)}, u32[]{:S(2)}, u32[]{:S(2)}) collective-permute-start(bf16[64,2048]{1,0:T(8,128)(2,1)S(1)} %get-tuple-element.26), channel_id=1, source_target_pairs={{0,64},{64,128},{128,192},{192,0},{1,65},{65,129},{129,193},{193,1... | collective-permute-start | bytes 786440 | tf_op jit(solution)/shard_map/ppermute | solution.py:275
  7.7 3.4 %early_attention.1 = f32[16,256]{1,0:T(8,128)S(1)} custom-call(s32[1,18]{1,0:T(1,128)S(1)} %get-tuple-element.25.info, bf16[1,512,2048]{2,1,0:T(8,128)(2,1)S(1)} %copy-done, bf16[1,2,512,128]{3,2,1,0:T(8,128)(2,1)S(1)} %copy-done.4, bf16[1,8,16,2048]{3,2,1,0:T(8,128)(2,1)S(1)} %copy-done.2), custom_call_target="tpu_custom_call" | custom-call | flops 587202560 | bytes 1572864 | tf_op jit(solution)/shard_map/early_attention/pallas_call | solution.py:330
  11.1 3.9 %collective-permute-start.6 = (bf16[1,512,2048]{2,1,0:T(8,128)(2,1)}, bf16[1,512,2048]{2,1,0:T(8,128)(2,1)}, u32[]{:S(2)}, u32[]{:S(2)}) collective-permute-start(bf16[1,512,2048]{2,1,0:T(8,128)(2,1)} %param.11), channel_id=1, source_target_pairs={{0,64},{64,128},{128,192},{192,0},{1,65},{65,129},{129,193},{193,1... | collective-permute-start | bytes 6291464 | tf_op jit(solution)/shard_map/ppermute | solution.py:275
  15.0 0.7 back_gradient.1
  15.8 0.1 collective-permute-start.1
  15.9 5.6 %collective-permute-done.1 = f32[16,512]{1,0:T(8,128)S(1)} collective-permute-done((f32[16,512]{1,0:T(8,128)S(1)}, f32[16,512]{1,0:T(8,128)S(1)}, u32[]{:S(2)}, u32[]{:S(2)}) %collective-permute-start.1) | collective-permute-done | bytes 32800 | tf_op jit(solution)/shard_map/ppermute | solution.py:275
  21.5 6.9 %collective-permute-start.2 = (f32[32,512]{1,0:T(8,128)S(1)}, f32[32,512]{1,0:T(8,128)S(1)}, u32[]{:S(2)}, u32[]{:S(2)}) collective-permute-start(f32[32,512]{1,0:T(8,128)S(1)} %pad_maximum_fusion), channel_id=1, source_target_pairs={{0,32},{8,40},{16,48},{24,56},{32,0},{40,8},{48,16},{56,24},{1,33}... | collective-permute-start | bytes 196616 | tf_op jit(solution)/shard_map/ppermute | solution.py:280
  28.4 3.4 %late_attention.1 = f32[16,256]{1,0:T(8,128)S(1)} custom-call(s32[1,18]{1,0:T(1,128)S(1)} %get-tuple-element.25.info, bf16[1,512,2048]{2,1,0:T(8,128)(2,1)S(1)} %copy-done, bf16[1,2,512,128]{3,2,1,0:T(8,128)(2,1)S(1)} %copy-done.4, bf16[1,8,16,2048]{3,2,1,0:T(8,128)(2,1)S(1)} %copy-done.2), custom_call_target="tpu_custom_call" | custom-call | flops 587202560 | bytes 1572864 | tf_op jit(solution)/shard_map/late_attention/pallas_call | solution.py:361
  31.9 0.7 broadcast_in_dim.2
  32.5 3.3 %all-to-all-start = ((bf16[4,32,512]{2,1,0:T(8,128)(2,1)}), bf16[4,32,512]{2,1,0:T(8,128)(2,1)S(1)}, u32[]{:S(2)}, u32[]{:S(2)}) async-start(bf16[4,32,512]{2,1,0:T(8,128)(2,1)} %broadcast_in_dim.2), calls=%async_computation | async-start | bytes 262144 | tf_op jit(solution)/shard_map/all_to_all | solution.py:372
  35.9 1.4 %collective-permute-start.3 = (f32[16,512]{1,0:T(8,128)S(1)}, f32[16,512]{1,0:T(8,128)S(1)}, u32[]{:S(2)}, u32[]{:S(2)}) collective-permute-start(f32[16,512]{1,0:T(8,128)S(1)} %constant_dynamic-update-slice_fusion), channel_id=1, source_target_pairs={{0,8},{8,0},{16,24},{24,16},{32,40},{40,32},{48,56},{56,48},{1,9},... | collective-permute-start | bytes 98312 | tf_op jit(solution)/shard_map/ppermute | solution.py:280
  37.3 2.3 %collective-permute-done.3 = f32[16,512]{1,0:T(8,128)S(1)} collective-permute-done((f32[16,512]{1,0:T(8,128)S(1)}, f32[16,512]{1,0:T(8,128)S(1)}, u32[]{:S(2)}, u32[]{:S(2)}) %collective-permute-start.3) | collective-permute-done | bytes 32800 | tf_op jit(solution)/shard_map/ppermute | solution.py:280
  39.6 1.4 %all-to-all-done.parts = bf16[4,32,512]{2,1,0:T(8,128)(2,1)S(1)} async-done(((bf16[4,32,512]{2,1,0:T(8,128)(2,1)}), bf16[4,32,512]{2,1,0:T(8,128)(2,1)S(1)}, u32[]{:S(2)}, u32[]{:S(2)}) %all-to-all-start) | async-done | bytes 131104 | tf_op jit(solution)/shard_map/all_to_all | solution.py:372
  41.0 4.0 %contract.1 = bf16[8,112,256]{2,1,0:T(8,128)(2,1)} custom-call(s32[1,18]{1,0:T(1,128)S(1)} %get-tuple-element.25.info, bf16[4,32,512]{2,1,0:T(8,128)(2,1)S(1)} %all-to-all-done.parts, bf16[64,2048]{1,0:T(8,128)(2,1)S(1)} %collective-permute-done.ahead, bf16[1,512,2048]{2,1,0:T(8,128)(2,1)} %saved.3, bf16[1,512,2048]{2,1,0:T(8,128)(2,1)} %grads.3), custom_call_target="tpu_custom_call" | custom-call | flops 201326592 | bytes 4194304 | tf_op jit(solution)/shard_map/contract/pallas_call | solution.py:376
  45.0 4.0 %all-to-all-start.1 = ((bf16[8,112,256]{2,1,0:T(8,128)(2,1)}), bf16[8,112,256]{2,1,0:T(8,128)(2,1)S(1)}, u32[]{:S(2)}, u32[]{:S(2)}) async-start(bf16[8,112,256]{2,1,0:T(8,128)(2,1)} %contract.1), calls=%async_computation.1 | async-start | bytes 917504 | tf_op jit(solution)/shard_map/all_to_all | solution.py:391
  49.0 1.7 %collective-permute-start.4 = (f32[16,512]{1,0:T(8,128)S(1)}, f32[16,512]{1,0:T(8,128)S(1)}, u32[]{:S(2)}, u32[]{:S(2)}) collective-permute-start(f32[16,512]{1,0:T(8,128)S(1)} %add.17), channel_id=1, source_target_pairs={{0,16},{8,24},{16,0},{24,8},{32,48},{40,56},{48,32},{56,40},{1,17}... | collective-permute-start | bytes 98312 | tf_op jit(solution)/shard_map/ppermute | solution.py:280
  50.7 2.6 %collective-permute-done.4 = f32[16,512]{1,0:T(8,128)S(1)} collective-permute-done((f32[16,512]{1,0:T(8,128)S(1)}, f32[16,512]{1,0:T(8,128)S(1)}, u32[]{:S(2)}, u32[]{:S(2)}) %collective-permute-start.4) | collective-permute-done | bytes 32800 | tf_op jit(solution)/shard_map/ppermute | solution.py:280
  53.3 4.7 %all-to-all-done.1.pieces = bf16[8,112,256]{2,1,0:T(8,128)(2,1)S(1)} async-done(((bf16[8,112,256]{2,1,0:T(8,128)(2,1)}), bf16[8,112,256]{2,1,0:T(8,128)(2,1)S(1)}, u32[]{:S(2)}, u32[]{:S(2)}) %all-to-all-start.1) | async-done | bytes 458784 | tf_op jit(solution)/shard_map/all_to_all | solution.py:391
  58.0 0.5 collect_up.1
  58.5 0.6 collective-permute-start.5
  59.1 1.4 %collect_down.1.half = bf16[8,256,256]{2,1,0:T(8,128)(2,1)} custom-call(bf16[8,112,256]{2,1,0:T(8,128)(2,1)S(1)} %all-to-all-done.1.pieces), custom_call_target="tpu_custom_call" | custom-call | flops 1572864 | bytes 1048576 | tf_op jit(solution)/shard_map/collect_down/pallas_call | solution.py:406
  60.5 0.0 copy-start.3
  60.5 3.2 %collective-permute-done.5.block = bf16[128,256]{1,0:T(8,128)(2,1)S(1)} collective-permute-done((bf16[128,256]{1,0:T(8,128)(2,1)S(1)}, bf16[128,256]{1,0:T(8,128)(2,1)S(1)}, u32[]{:S(2)}, u32[]{:S(2)}) %collective-permute-start.5) | collective-permute-done | bytes 65568 | tf_op jit(solution)/shard_map/ppermute | solution.py:275
  63.7 0.9 %add_up.1 = bf16[8,256,256]{2,1,0:T(8,128)(2,1)} custom-call(bf16[128,256]{1,0:T(8,128)(2,1)S(1)} %collective-permute-done.5.block, bf16[8,256,256]{2,1,0:T(8,128)(2,1)} %collect_down.1.half), custom_call_target="tpu_custom_call", output_to_operand_aliasing={{}: (1, {})} | custom-call | bytes 524288 | tf_op jit(solution)/shard_map/add_up/pallas_call | solution.py:416
  64.6 3.6 %all-to-all-start.2 = ((bf16[8,256,256]{2,1,0:T(8,128)(2,1)}), bf16[8,256,256]{2,1,0:T(8,128)(2,1)S(1)}, u32[]{:S(2)}, u32[]{:S(2)}) async-start(bf16[8,256,256]{2,1,0:T(8,128)(2,1)} %add_up.1), calls=%async_computation.2 | async-start | bytes 2097152 | tf_op jit(solution)/shard_map/all_to_all | solution.py:429
  68.2 4.0 %collective-permute-start.7 = (f32[16,512]{1,0:T(8,128)S(1)}, f32[16,512]{1,0:T(8,128)S(1)}, u32[]{:S(2)}, u32[]{:S(2)}) collective-permute-start(f32[16,512]{1,0:T(8,128)S(1)} %add.18), channel_id=1, source_target_pairs={{0,32},{8,40},{16,48},{24,56},{32,0},{40,8},{48,16},{56,24},{1,33}... | collective-permute-start | bytes 98312 | tf_op jit(solution)/shard_map/ppermute | solution.py:280
  72.2 2.8 %collective-permute-done.7 = f32[16,512]{1,0:T(8,128)S(1)} collective-permute-done((f32[16,512]{1,0:T(8,128)S(1)}, f32[16,512]{1,0:T(8,128)S(1)}, u32[]{:S(2)}, u32[]{:S(2)}) %collective-permute-start.7) | collective-permute-done | bytes 32800 | tf_op jit(solution)/shard_map/ppermute | solution.py:280
  75.0 4.4 %hand_on.1 = bf16[1,512,2048]{2,1,0:T(8,128)(2,1)} custom-call(s32[1,18]{1,0:T(1,128)S(1)} %get-tuple-element.25.info, bf16[1,512,2048]{2,1,0:T(8,128)(2,1)} %collective-permute-done.6.arrived, f32[16,512]{1,0:T(8,128)S(1)} %add.19.fwd, bf16[1,8,16,2048]{3,2,1,0:T(8,128)(2,1)S(1)} %copy-done.3), custom_call_target="tpu_custom_call" | custom-call | flops 100663296 | bytes 4194304 | tf_op jit(solution)/shard_map/hand_on/pallas_call | solution.py:432
  79.4 3.1 %all-to-all-done.2.sums = bf16[8,256,256]{2,1,0:T(8,128)(2,1)S(1)} async-done(((bf16[8,256,256]{2,1,0:T(8,128)(2,1)}), bf16[8,256,256]{2,1,0:T(8,128)(2,1)S(1)}, u32[]{:S(2)}, u32[]{:S(2)}) %all-to-all-start.2) | async-done | bytes 1048608 | tf_op jit(solution)/shard_map/all_to_all | solution.py:429
  82.5 1.1 %unpack.1 = (bf16[1,8,16,2048]{3,2,1,0:T(8,128)(2,1)}, bf16[1,8,16,2048]{3,2,1,0:T(8,128)(2,1)}) custom-call(bf16[8,256,256]{2,1,0:T(8,128)(2,1)S(1)} %all-to-all-done.2.sums), custom_call_target="tpu_custom_call" | custom-call | bytes 2097152 | tf_op jit(solution)/shard_map/unpack/pallas_call | solution.py:444
  (19 shorter events, 0.1 us)
Async XLA Ops:
  0.6 7.1 %copy-start.2 = (bf16[1,8,16,2048]{3,2,1,0:T(8,128)(2,1)S(1)}, bf16[1,8,16,2048]{3,2,1,0:T(8,128)(2,1)}, u32[]{:S(2)}) copy-start(bf16[1,8,16,2048]{3,2,1,0:T(8,128)(2,1)} %down.5) | copy-start | bytes 1572868
  0.6 7.1 %copy-start.4 = (bf16[1,2,512,128]{3,2,1,0:T(8,128)(2,1)S(1)}, bf16[1,2,512,128]{3,2,1,0:T(8,128)(2,1)}, u32[]{:S(2)}) copy-start(bf16[1,2,512,128]{3,2,1,0:T(8,128)(2,1)} %keys_values.3) | copy-start | bytes 786436
  0.7 7.1 %copy-start = (bf16[1,512,2048]{2,1,0:T(8,128)(2,1)S(1)}, bf16[1,512,2048]{2,1,0:T(8,128)(2,1)}, u32[]{:S(2)}) copy-start(bf16[1,512,2048]{2,1,0:T(8,128)(2,1)} %queries.2) | copy-start | bytes 6291460
  3.5 11.5 %copy-start.1 = (bf16[1,512,2048]{2,1,0:T(8,128)(2,1)S(1)}, bf16[1,512,2048]{2,1,0:T(8,128)(2,1)}, u32[]{:S(2)}) copy-start(bf16[1,512,2048]{2,1,0:T(8,128)(2,1)} %grads.3) | copy-start | bytes 6291460
  3.5 7.6 %collective-permute-start = (bf16[64,2048]{1,0:T(8,128)(2,1)S(1)}, bf16[64,2048]{1,0:T(8,128)(2,1)S(1)}, u32[]{:S(2)}, u32[]{:S(2)}) collective-permute-start(bf16[64,2048]{1,0:T(8,128)(2,1)S(1)} %get-tuple-element.26), channel_id=1, source_target_pairs={{0,64},{64,128},{128,192},{192,0},{1,65},{65,129},{129,193},{193,1... | collective-permute-start | bytes 786440 | tf_op jit(solution)/shard_map/ppermute | solution.py:275
  11.1 53.5 %collective-permute-start.6 = (bf16[1,512,2048]{2,1,0:T(8,128)(2,1)}, bf16[1,512,2048]{2,1,0:T(8,128)(2,1)}, u32[]{:S(2)}, u32[]{:S(2)}) collective-permute-start(bf16[1,512,2048]{2,1,0:T(8,128)(2,1)} %param.11), channel_id=1, source_target_pairs={{0,64},{64,128},{128,192},{192,0},{1,65},{65,129},{129,193},{193,1... | collective-permute-start | bytes 6291464 | tf_op jit(solution)/shard_map/ppermute | solution.py:275
  15.8 5.7 %collective-permute-start.1 = (f32[16,512]{1,0:T(8,128)S(1)}, f32[16,512]{1,0:T(8,128)S(1)}, u32[]{:S(2)}, u32[]{:S(2)}) collective-permute-start(f32[16,512]{1,0:T(8,128)S(1)} %back_gradient.1), channel_id=1, source_target_pairs={{0,192},{64,0},{128,64},{192,128},{1,193},{65,1},{129,65},{193,129... | collective-permute-start | bytes 98312 | tf_op jit(solution)/shard_map/ppermute | solution.py:275
  21.5 10.3 %collective-permute-start.2 = (f32[32,512]{1,0:T(8,128)S(1)}, f32[32,512]{1,0:T(8,128)S(1)}, u32[]{:S(2)}, u32[]{:S(2)}) collective-permute-start(f32[32,512]{1,0:T(8,128)S(1)} %pad_maximum_fusion), channel_id=1, source_target_pairs={{0,32},{8,40},{16,48},{24,56},{32,0},{40,8},{48,16},{56,24},{1,33}... | collective-permute-start | bytes 196616 | tf_op jit(solution)/shard_map/ppermute | solution.py:280
  32.5 8.5 %all-to-all-start = ((bf16[4,32,512]{2,1,0:T(8,128)(2,1)}), bf16[4,32,512]{2,1,0:T(8,128)(2,1)S(1)}, u32[]{:S(2)}, u32[]{:S(2)}) async-start(bf16[4,32,512]{2,1,0:T(8,128)(2,1)} %broadcast_in_dim.2), calls=%async_computation | async-start | bytes 262144 | tf_op jit(solution)/shard_map/all_to_all | solution.py:372
  35.9 3.7 %collective-permute-start.3 = (f32[16,512]{1,0:T(8,128)S(1)}, f32[16,512]{1,0:T(8,128)S(1)}, u32[]{:S(2)}, u32[]{:S(2)}) collective-permute-start(f32[16,512]{1,0:T(8,128)S(1)} %constant_dynamic-update-slice_fusion), channel_id=1, source_target_pairs={{0,8},{8,0},{16,24},{24,16},{32,40},{40,32},{48,56},{56,48},{1,9},... | collective-permute-start | bytes 98312 | tf_op jit(solution)/shard_map/ppermute | solution.py:280
  45.0 13.0 %all-to-all-start.1 = ((bf16[8,112,256]{2,1,0:T(8,128)(2,1)}), bf16[8,112,256]{2,1,0:T(8,128)(2,1)S(1)}, u32[]{:S(2)}, u32[]{:S(2)}) async-start(bf16[8,112,256]{2,1,0:T(8,128)(2,1)} %contract.1), calls=%async_computation.1 | async-start | bytes 917504 | tf_op jit(solution)/shard_map/all_to_all | solution.py:391
  49.0 4.3 %collective-permute-start.4 = (f32[16,512]{1,0:T(8,128)S(1)}, f32[16,512]{1,0:T(8,128)S(1)}, u32[]{:S(2)}, u32[]{:S(2)}) collective-permute-start(f32[16,512]{1,0:T(8,128)S(1)} %add.17), channel_id=1, source_target_pairs={{0,16},{8,24},{16,0},{24,8},{32,48},{40,56},{48,32},{56,40},{1,17}... | collective-permute-start | bytes 98312 | tf_op jit(solution)/shard_map/ppermute | solution.py:280
  58.5 5.3 %collective-permute-start.5 = (bf16[128,256]{1,0:T(8,128)(2,1)S(1)}, bf16[128,256]{1,0:T(8,128)(2,1)S(1)}, u32[]{:S(2)}, u32[]{:S(2)}) collective-permute-start(bf16[128,256]{1,0:T(8,128)(2,1)S(1)} %collect_up.1), channel_id=1, source_target_pairs={{0,192},{64,0},{128,64},{192,128},{1,193},{65,1},{129,65},{193,129... | collective-permute-start | bytes 196616 | tf_op jit(solution)/shard_map/ppermute | solution.py:275
  60.5 14.5 %copy-start.3 = (bf16[1,8,16,2048]{3,2,1,0:T(8,128)(2,1)S(1)}, bf16[1,8,16,2048]{3,2,1,0:T(8,128)(2,1)}, u32[]{:S(2)}) copy-start(bf16[1,8,16,2048]{3,2,1,0:T(8,128)(2,1)} %up.3) | copy-start | bytes 1572868
  64.6 17.9 %all-to-all-start.2 = ((bf16[8,256,256]{2,1,0:T(8,128)(2,1)}), bf16[8,256,256]{2,1,0:T(8,128)(2,1)S(1)}, u32[]{:S(2)}, u32[]{:S(2)}) async-start(bf16[8,256,256]{2,1,0:T(8,128)(2,1)} %add_up.1), calls=%async_computation.2 | async-start | bytes 2097152 | tf_op jit(solution)/shard_map/all_to_all | solution.py:429
  68.2 6.8 %collective-permute-start.7 = (f32[16,512]{1,0:T(8,128)S(1)}, f32[16,512]{1,0:T(8,128)S(1)}, u32[]{:S(2)}, u32[]{:S(2)}) collective-permute-start(f32[16,512]{1,0:T(8,128)S(1)} %add.18), channel_id=1, source_target_pairs={{0,32},{8,40},{16,48},{24,56},{32,0},{40,8},{48,16},{56,24},{1,33}... | collective-permute-start | bytes 98312 | tf_op jit(solution)/shard_map/ppermute | solution.py:280
